TPU v7x, 128 devices: a whole 4x4x4 slice. The times are simulated.
128 devices in a mesh: ctx: 16 (over y, x_hi, core), fsdp: 8 (over x_lo, z).
Axes of the slice: x: 4 (x_hi: 2, x_lo: 2; x = x_hi * 2 + x_lo), y: 4, z: 4, core: 2. Of those that a mesh axis runs over, the one named last changes fastest.
Arguments:
- tokens: bfloat16 [8, 2048, 1024], P('fsdp', 'ctx'), may hold values from -6 to 6
- block_order: int32 [16], replicated, may hold values from 0 to 15, each once
- routes: int32 [8, 2048, 8], P('fsdp', 'ctx'), may hold values from 0 to 9, all different within a row; in each aligned block of 128 rows (0 to 127, 128 to 255, ..., all dimensions but the last counted through in order) at most 128 rows name the same one
- attn_gain: bfloat16 [1024], P('fsdp'), may hold values from 0.5 to 1.5
- qkv_weight: bfloat16 [1024, 2048], P('fsdp'), may hold values from -0.1875 to 0.1875
- proj_weight: bfloat16 [1024, 1024], P('fsdp'), may hold values from -3 to 3
- moe_gain: bfloat16 [1024], P('fsdp'), may hold values from 0.5 to 1.5
- router_weight: bfloat16 [1024, 10], P('fsdp'), may hold values from -0.09375 to 0.09375
- expert_in: bfloat16 [1024, 10, 1024], P('fsdp'), may hold values from -0.1875 to 0.1875
- expert_down: bfloat16 [1024, 10, 512], P('fsdp'), may hold values from -1 to 1
- cotangent: bfloat16 [8, 2048, 1024], P('fsdp', 'ctx'), may hold values from -6 to 6
Outputs:
- layer_out: bfloat16 [8, 2048, 1024], P('fsdp', 'ctx')
- tokens_grad: float32 [8, 2048, 1024], P('fsdp', 'ctx')
- attn_gain_grad: float32 [1024], P('fsdp')
- qkv_grad: float32 [1024, 2048], P('fsdp')
- proj_grad: float32 [1024, 1024], P('fsdp')
- moe_gain_grad: float32 [1024], P('fsdp')
- router_grad: float32 [1024, 10], P('fsdp')
- expert_in_grad: float32 [1024, 10, 1024], P('fsdp')
- expert_down_grad: float32 [1024, 10, 512], P('fsdp')
Inputs may be any that keep to these rules, and one draw needn't show every extreme that they name: `block_order`: a permutation of the indices of ctx. `routes`: each row names 8 different experts; in each device's 128 rows no expert is named more than 128 times, a bound that some block reaches there in some devices' rows.
All inputs are finite; a program needn't handle non-finite values.
Results may differ from a plain program's by a relative error of at most 0.025.
Values may be sent and summed in bfloat16 or wider, within the bound.
No kernel may reach another device: no remote copies, remote signals or barrier semaphores. Data moves between devices by JAX's collectives and lax.ppermute only.
A program may use at most 192 MiB of HBM per device.

v0:
```python
import math

import jax
import jax.numpy as jnp
from jax import lax
from jax.sharding import PartitionSpec as P

HEADS = 16
KV_HEADS = 8
HEAD_DIM = 64
CAPACITY = 128


EPSILON = 1e-06
THETA = 10000.0
NEGATIVE = -1e30


def rms_scale(values):
    return lax.rsqrt(jnp.mean(values * values, axis=-1, keepdims=True) + EPSILON)


def slot_positions(orders, per_device, blocks):
    within = jnp.arange(per_device, dtype=jnp.int32)
    halfway = per_device // 2
    first = within < halfway
    placed = jnp.where(first[None, :], orders[:, None], blocks - 1 - orders[:, None])
    return placed * halfway + within[None, :] % halfway


def rotary_tables(positions, head_size):
    halfway = head_size // 2
    frequency = THETA ** (-(jnp.arange(halfway, dtype=jnp.float32) * 2.0) / head_size)
    angles = positions.astype(jnp.float32)[:, None] * frequency[None, :]
    return (jnp.cos(angles)[:, None, :], jnp.sin(angles)[:, None, :])


def rotate(values, cos_table, sin_table):
    halfway = values.shape[-1] // 2
    first_half = values[..., :halfway]
    second_half = values[..., halfway:]
    return jnp.concatenate(
        [
            first_half * cos_table - second_half * sin_table,
            second_half * cos_table + first_half * sin_table,
        ],
        axis=-1,
    )


def unrotate(values, cos_table, sin_table):
    halfway = values.shape[-1] // 2
    first_half = values[..., :halfway]
    second_half = values[..., halfway:]
    return jnp.concatenate(
        [
            first_half * cos_table + second_half * sin_table,
            second_half * cos_table - first_half * sin_table,
        ],
        axis=-1,
    )


def group_rows(values, kv_count):
    length, head_count, head_size = values.shape
    group_size = head_count // kv_count
    arranged = values.reshape(length, kv_count, group_size, head_size).transpose(1, 2, 0, 3)
    return arranged.reshape(kv_count, group_size * length, head_size)


def ungroup_rows(values, head_count):
    kv_count, rows_all, head_size = values.shape
    group_size = head_count // kv_count
    length = rows_all // group_size
    arranged = values.reshape(kv_count, group_size, length, head_size).transpose(2, 0, 1, 3)
    return arranged.reshape(length, head_count * head_size)


def reduce_rows(lefts, rights, term):
    return lax.psum_scatter(
        term(tuple((array for array in lefts)), rights).astype(jnp.bfloat16),
        "fsdp",
        scatter_dimension=0,
        tiled=True,
    ).astype(jnp.float32)


def body(
    tokens,
    block_order,
    routes,
    attn_gain,
    qkv_weight,
    proj_weight,
    moe_gain,
    router_weight,
    expert_in,
    expert_down,
    cotangent,
):
    ctx_count = lax.axis_size("ctx")
    model_width = tokens.shape[2]
    local_rows = tokens.shape[1]
    seq_length = local_rows * ctx_count
    head_size = HEAD_DIM
    head_count = HEADS
    kv_count = KV_HEADS
    group_size = head_count // kv_count
    query_width = head_count * head_size
    kv_width = kv_count * head_size
    expert_count = expert_in.shape[1]
    hidden_width = expert_down.shape[2]
    top_count = routes.shape[2]
    capacity = CAPACITY
    score_scale = 1.0 / math.sqrt(head_size)
    residual_stream = tokens.reshape(local_rows, model_width).astype(jnp.float32)
    upstream = cotangent.reshape(local_rows, model_width).astype(jnp.float32)
    route_rows = routes.reshape(local_rows, top_count)
    ctx_ids = jnp.arange(ctx_count, dtype=jnp.int32)
    own_order = jnp.sum(jnp.where(ctx_ids == lax.axis_index("ctx"), block_order, 0))
    query_pos = slot_positions(own_order[None], local_rows, 2 * ctx_count).reshape(local_rows)
    key_pos = slot_positions(block_order, local_rows, 2 * ctx_count).reshape(seq_length)
    cos_table, sin_table = rotary_tables(query_pos, head_size)
    qkv_full, proj_full, gain_full = (
        lax.all_gather(qkv_weight, "fsdp", axis=0, tiled=True),
        lax.all_gather(proj_weight, "fsdp", axis=0, tiled=True),
        lax.all_gather(attn_gain, "fsdp", axis=0, tiled=True),
    )
    gain_one = gain_full.astype(jnp.float32)
    first_inverse_deviation = rms_scale(residual_stream)
    normed_one = (residual_stream * first_inverse_deviation * gain_one).astype(jnp.bfloat16)
    projected = jnp.dot(normed_one, qkv_full, preferred_element_type=jnp.float32)
    queries = rotate(
        projected[:, :query_width].reshape(local_rows, head_count, head_size), cos_table, sin_table
    ).astype(jnp.bfloat16)
    key_local = (
        rotate(
            projected[:, query_width : query_width + kv_width].reshape(
                local_rows, kv_count, head_size
            ),
            cos_table,
            sin_table,
        )
        .astype(jnp.bfloat16)
        .reshape(local_rows, kv_width)
    )
    value_local = projected[:, query_width + kv_width :].astype(jnp.bfloat16)
    keys_all, values_all = (
        lax.all_gather(key_local, "ctx", axis=0, tiled=True),
        lax.all_gather(value_local, "ctx", axis=0, tiled=True),
    )
    key_block = math.gcd(512, seq_length)
    block_count = seq_length // key_block
    keys_split = keys_all.reshape(block_count, key_block, kv_count, head_size).transpose(0, 2, 1, 3)
    values_split = values_all.reshape(block_count, key_block, kv_count, head_size).transpose(
        0, 2, 1, 3
    )
    key_pos_split = key_pos.reshape(block_count, key_block)
    grouped = group_rows(queries, kv_count)
    row_pos = jnp.tile(query_pos, group_size)
    rows_grouped = grouped.shape[1]
    tiles = (keys_split, values_split, key_pos_split)

    def masked_scores(key_tile, tile_pos):
        scores = (
            jnp.einsum("grd,gkd->grk", grouped, key_tile, preferred_element_type=jnp.float32)
            * score_scale
        )
        visible = tile_pos[None, None, :] <= row_pos[None, :, None]
        return (jnp.where(visible, scores, NEGATIVE), visible)

    def lse_step(carried, element):
        running, totals = carried
        key_tile, value_tile, tile_pos = element
        masked, visible = masked_scores(key_tile, tile_pos)
        largest = jnp.maximum(running, jnp.max(masked, axis=-1))
        exponent = jnp.where(visible, jnp.exp(masked - largest[..., None]), 0.0)
        totals = totals * jnp.exp(running - largest) + jnp.sum(exponent, axis=-1)
        return ((largest, totals), None)

    start_max = jnp.full((kv_count, rows_grouped), NEGATIVE, jnp.float32)
    (running_max, running_sum), _ = lax.scan(
        lse_step, (start_max, jnp.zeros_like(start_max)), tiles
    )
    log_total = running_max + jnp.log(running_sum)

    def probs_of(key_tile, tile_pos):
        masked, visible = masked_scores(key_tile, tile_pos)
        return jnp.where(visible, jnp.exp(masked - log_total[..., None]), 0.0)

    def output_step(accumulated, element):
        key_tile, value_tile, tile_pos = element
        weights_tile = probs_of(key_tile, tile_pos).astype(jnp.bfloat16)
        return (
            accumulated
            + jnp.einsum(
                "grk,gkd->grd", weights_tile, value_tile, preferred_element_type=jnp.float32
            ),
            None,
        )

    attended_grouped, _ = lax.scan(
        output_step, jnp.zeros((kv_count, rows_grouped, head_size), jnp.float32), tiles
    )
    attended = ungroup_rows(attended_grouped, head_count).astype(jnp.bfloat16)
    hidden_state = residual_stream + jnp.einsum(
        "ti,di->td", attended, proj_full, preferred_element_type=jnp.float32
    )
    expert_ids = jnp.arange(expert_count, dtype=jnp.int32)
    picked = route_rows[:, :, None] == expert_ids[None, None, :]
    chosen = jnp.sum(picked.astype(jnp.int32), axis=1)
    earlier = jnp.cumsum(chosen, axis=0) - chosen
    slot_ids = jnp.arange(capacity, dtype=jnp.int32)
    dispatch_grid = (chosen.T[:, None, :] == 1) & (earlier.T[:, None, :] == slot_ids[None, :, None])
    dispatch = dispatch_grid.astype(jnp.bfloat16).reshape(expert_count * capacity, local_rows)
    slot_index = jnp.sum(jnp.where(picked, earlier[:, None, :], 0), axis=2)
    flat_index = route_rows * capacity + slot_index
    second_inverse_deviation = rms_scale(hidden_state)
    in_piece = lax.all_gather(expert_in, "fsdp", axis=0, tiled=True)
    router_piece = lax.all_gather(router_weight, "fsdp", axis=0, tiled=True)
    gain_piece = lax.all_gather(moe_gain, "fsdp", axis=0, tiled=True)
    piece_width = in_piece.shape[0]
    gain_part = gain_piece.astype(jnp.float32)
    normed_part = (hidden_state * second_inverse_deviation * gain_part).astype(jnp.bfloat16)
    slot_part = (
        jnp.dot(dispatch, normed_part, preferred_element_type=jnp.float32)
        .astype(jnp.bfloat16)
        .reshape(expert_count, capacity, piece_width)
    )
    gate_up = jnp.einsum("eck,kef->ecf", slot_part, in_piece, preferred_element_type=jnp.float32)
    logits = jnp.dot(normed_part, router_piece, preferred_element_type=jnp.float32)
    slot_rows = slot_part
    normed_two = normed_part
    gain_two = gain_part
    gate_up, logits, slot_rows, normed_two, gain_two = (
        gate_up,
        logits,
        slot_rows,
        normed_two,
        gain_two,
    )
    gate_pre = gate_up[..., :hidden_width]
    up_pre = gate_up[..., hidden_width:]
    sigmoid_gate = jax.nn.sigmoid(gate_pre)
    silu_gate = gate_pre * sigmoid_gate
    act = (silu_gate * up_pre).astype(jnp.bfloat16)
    expert_rows = jnp.einsum(
        "ecf,kef->eck",
        act,
        lax.all_gather(expert_down, "fsdp", axis=0, tiled=True),
        preferred_element_type=jnp.float32,
    ).astype(jnp.bfloat16)
    token_rows = expert_rows.reshape(expert_count * capacity, model_width)[flat_index].astype(
        jnp.float32
    )
    chosen_logits = jnp.sum(jnp.where(picked, logits[:, None, :], 0.0), axis=2)
    largest_logit = jnp.max(chosen_logits, axis=-1, keepdims=True)
    exponent_logit = jnp.exp(chosen_logits - largest_logit)
    gate_weights = exponent_logit / jnp.sum(exponent_logit, axis=-1, keepdims=True)
    block_out = hidden_state + jnp.einsum("tk,tkd->td", gate_weights, token_rows)
    layer_out = block_out.astype(jnp.bfloat16).reshape(1, local_rows, model_width)
    grad_gates = jnp.einsum("td,tkd->tk", upstream, token_rows)
    grad_chosen = gate_weights * (
        grad_gates - jnp.sum(gate_weights * grad_gates, axis=-1, keepdims=True)
    )
    grad_logits = jnp.sum(jnp.where(picked, grad_chosen[:, :, None], 0.0), axis=1).astype(
        jnp.bfloat16
    )
    token_grads = (
        (gate_weights[:, :, None] * upstream[:, None, :])
        .astype(jnp.bfloat16)
        .reshape(local_rows * top_count, model_width)
    )
    grad_rows = (
        jnp.zeros((expert_count * capacity, model_width), jnp.bfloat16)
        .at[flat_index.reshape(local_rows * top_count)]
        .set(token_grads)
        .reshape(expert_count, capacity, model_width)
    )
    piece_rows = lax.all_gather(expert_down, "fsdp", axis=0, tiled=True)
    grad_act = jnp.einsum("eck,kef->ecf", grad_rows, piece_rows, preferred_element_type=jnp.float32)
    grad_gate = grad_act * up_pre * sigmoid_gate * (1.0 + gate_pre * (1.0 - sigmoid_gate))
    grad_up = grad_act * silu_gate
    grad_pre = jnp.concatenate([grad_gate, grad_up], axis=-1).astype(jnp.bfloat16)
    in_piece = lax.all_gather(expert_in, "fsdp", axis=0, tiled=True)
    router_piece = lax.all_gather(router_weight, "fsdp", axis=0, tiled=True)
    slot_cols = jnp.einsum("ecf,kef->eck", grad_pre, in_piece, preferred_element_type=jnp.float32)
    router_cols = jnp.einsum(
        "te,ke->tk", grad_logits, router_piece, preferred_element_type=jnp.float32
    )
    slot_grad = slot_cols
    router_part = router_cols
    slot_grad, router_part = (slot_grad, router_part)
    second_normalized_gradient = (
        jnp.sum(slot_grad.reshape(expert_count * capacity, model_width)[flat_index], axis=1)
        + router_part
    )

    def pair_term(parts, others):
        return jnp.einsum("eck,ecf->kef", parts[0], others[0], preferred_element_type=jnp.float32)

    down_rows = reduce_rows((grad_rows,), (act,), pair_term)
    in_rows = reduce_rows((slot_rows,), (grad_pre,), pair_term)
    router_term = jnp.einsum(
        "td,te->de", normed_two, grad_logits, preferred_element_type=jnp.float32
    )
    second_normalized_input = hidden_state * second_inverse_deviation
    second_gain_gradient = jnp.sum(second_normalized_gradient * second_normalized_input, axis=0)
    second_scaled_input = second_normalized_gradient * gain_two
    grad_hidden = upstream + second_inverse_deviation * (
        second_scaled_input
        - second_normalized_input
        * jnp.mean(second_scaled_input * second_normalized_input, axis=-1, keepdims=True)
    )
    qkv_back, proj_back = (
        lax.all_gather(qkv_weight, "fsdp", axis=0, tiled=True),
        lax.all_gather(proj_weight, "fsdp", axis=0, tiled=True),
    )
    grad_branch = grad_hidden.astype(jnp.bfloat16)
    grad_attended = jnp.dot(grad_branch, proj_back, preferred_element_type=jnp.float32).astype(
        jnp.bfloat16
    )
    grad_grouped = group_rows(grad_attended.reshape(local_rows, head_count, head_size), kv_count)

    def correction_step(totals, element):
        key_tile, value_tile, tile_pos = element
        weights_tile = probs_of(key_tile, tile_pos)
        grad_probs = jnp.einsum(
            "grd,gkd->grk", grad_grouped, value_tile, preferred_element_type=jnp.float32
        )
        return (totals + jnp.sum(weights_tile * grad_probs, axis=-1), None)

    correction, _ = lax.scan(
        correction_step, jnp.zeros((kv_count, rows_grouped), jnp.float32), tiles
    )

    def grad_step(accumulated, element):
        key_tile, value_tile, tile_pos = element
        weights_tile = probs_of(key_tile, tile_pos)
        grad_probs = jnp.einsum(
            "grd,gkd->grk", grad_grouped, value_tile, preferred_element_type=jnp.float32
        )
        grad_scores = (weights_tile * (grad_probs - correction[..., None])).astype(jnp.bfloat16)
        accumulated = (
            accumulated
            + jnp.einsum("grk,gkd->grd", grad_scores, key_tile, preferred_element_type=jnp.float32)
            * score_scale
        )
        key_part = (
            jnp.einsum("grk,grd->gkd", grad_scores, grouped, preferred_element_type=jnp.float32)
            * score_scale
        )
        value_part = jnp.einsum(
            "grk,grd->gkd",
            weights_tile.astype(jnp.bfloat16),
            grad_grouped,
            preferred_element_type=jnp.float32,
        )
        return (accumulated, (key_part, value_part))

    grad_query_grouped, (key_parts, value_parts) = lax.scan(
        grad_step, jnp.zeros((kv_count, rows_grouped, head_size), jnp.float32), tiles
    )
    key_terms = key_parts.transpose(0, 2, 1, 3).reshape(seq_length, kv_width)
    value_terms = value_parts.transpose(0, 2, 1, 3).reshape(seq_length, kv_width)
    key_grad, value_grad = (
        lax.psum_scatter(
            key_terms.astype(jnp.bfloat16), "ctx", scatter_dimension=0, tiled=True
        ).astype(jnp.float32),
        lax.psum_scatter(
            value_terms.astype(jnp.bfloat16), "ctx", scatter_dimension=0, tiled=True
        ).astype(jnp.float32),
    )
    grad_query = unrotate(
        ungroup_rows(grad_query_grouped, head_count).reshape(local_rows, head_count, head_size),
        cos_table,
        sin_table,
    ).reshape(local_rows, query_width)
    grad_key = unrotate(
        key_grad.reshape(local_rows, kv_count, head_size), cos_table, sin_table
    ).reshape(local_rows, kv_width)
    grad_mixed = jnp.concatenate([grad_query, grad_key, value_grad], axis=1).astype(jnp.bfloat16)
    first_normalized_gradient = jnp.einsum(
        "tj,dj->td", grad_mixed, qkv_back, preferred_element_type=jnp.float32
    )

    def attn_term(parts, others):
        qkv_part = jnp.einsum(
            "etk,etj->kj", parts[0], others[0], preferred_element_type=jnp.float32
        )
        proj_part = jnp.einsum(
            "etk,etj->kj", parts[1], others[1], preferred_element_type=jnp.float32
        )
        return jnp.concatenate([qkv_part, proj_part], axis=1)

    qkv_columns = qkv_weight.shape[1]
    attn_rows = reduce_rows(
        (normed_one[None], grad_branch[None]), (grad_mixed[None], attended[None]), attn_term
    )
    first_normalized_input = residual_stream * first_inverse_deviation
    first_gain_gradient = jnp.sum(first_normalized_gradient * first_normalized_input, axis=0)
    first_scaled_input = first_normalized_gradient * gain_one
    tokens_grad = grad_hidden + first_inverse_deviation * (
        first_scaled_input
        - first_normalized_input
        * jnp.mean(first_scaled_input * first_normalized_input, axis=-1, keepdims=True)
    )
    small_one, small_two, small_router = (
        lax.psum_scatter(
            first_gain_gradient.astype(jnp.bfloat16), "fsdp", scatter_dimension=0, tiled=True
        ).astype(jnp.float32),
        lax.psum_scatter(
            second_gain_gradient.astype(jnp.bfloat16), "fsdp", scatter_dimension=0, tiled=True
        ).astype(jnp.float32),
        lax.psum_scatter(
            router_term.astype(jnp.bfloat16), "fsdp", scatter_dimension=0, tiled=True
        ).astype(jnp.float32),
    )
    summed = (
        lax.psum(attn_rows.astype(jnp.bfloat16), "ctx").astype(jnp.float32),
        lax.psum(in_rows.astype(jnp.bfloat16), "ctx").astype(jnp.float32),
        lax.psum(down_rows.astype(jnp.bfloat16), "ctx").astype(jnp.float32),
        lax.psum(small_one.astype(jnp.bfloat16), "ctx").astype(jnp.float32),
        lax.psum(small_two.astype(jnp.bfloat16), "ctx").astype(jnp.float32),
        lax.psum(small_router.astype(jnp.bfloat16), "ctx").astype(jnp.float32),
    )
    qkv_grad = summed[0][:, :qkv_columns]
    proj_grad = summed[0][:, qkv_columns:]
    return (
        layer_out,
        tokens_grad.reshape(1, local_rows, model_width),
        summed[3],
        qkv_grad,
        proj_grad,
        summed[4],
        summed[5],
        summed[1],
        summed[2],
    )


def solution(mesh):
    in_specs = (
        P("fsdp", "ctx", None),
        P(),
        P("fsdp", "ctx", None),
        P("fsdp"),
        P("fsdp", None),
        P("fsdp", None),
        P("fsdp"),
        P("fsdp", None),
        P("fsdp", None, None),
        P("fsdp", None, None),
        P("fsdp", "ctx", None),
    )
    out_specs = (
        P("fsdp", "ctx", None),
        P("fsdp", "ctx", None),
        P("fsdp"),
        P("fsdp", None),
        P("fsdp", None),
        P("fsdp"),
        P("fsdp", None),
        P("fsdp", None, None),
        P("fsdp", None, None),
    )
    return jax.shard_map(body, mesh=mesh, in_specs=in_specs, out_specs=out_specs, check_vma=False)
```

profile of v0, /device:TPU:1, one launch (start us, length us, event | category | flops | bytes accessed | tf_op | source)
XLA Modules:
  0.0 1431.6 jit_solution(10949701733740360909)
XLA Ops:
  8.0 17.2 %all-gather = bf16[8,1,128]{2,1,0:T(2,128)(2,1)S(1)} all-gather(bf16[1,1,128]{2,1,0:T(2,128)(2,1)} %bitcast.437), channel_id=1, replica_groups=mesh['ctx'=16,'fsdp'=8] {'fsdp'}, dimensions={0}, use_global_device_ids=true | all-gather | bytes 2304 | tf_op jit(solution)/shard_map/all_gather | solution.py:127
  29.0 36.7 %all-gather.9.cloned.1.call-done = bf16[1024,2048]{1,0:T(8,128)(2,1)} async-done(((bf16[128,2048]{1,0:T(8,128)(2,1)}), bf16[1024,2048]{1,0:T(8,128)(2,1)}) %all-gather.9.cloned.1.call-update) | async-done | bytes 4194320 | tf_op jit(solution)/shard_map/all_gather | solution.py:125
  72.5 12.0 all-gather.1
  86.5 19.4 %all_gather.38 = bf16[1024,10]{0,1:T(8,128)(2,1)S(1)} all-gather(bf16[128,10]{0,1:T(8,128)(2,1)S(1)} %copy-done.37), channel_id=1, replica_groups=mesh['ctx'=16,'fsdp'=8] {'fsdp'}, dimensions={0}, use_global_device_ids=true | all-gather | bytes 23040 | tf_op jit(solution)/shard_map/all_gather | solution.py:220
  107.3 8.5 all-gather.11.cloned.1.call-done
  122.5 42.0 %all-gather.13.cloned.1.call-done = bf16[2048,512]{1,0:T(8,128)(2,1)} async-done(((bf16[128,512]{1,0:T(8,128)(2,1)}), bf16[2048,512]{1,0:T(8,128)(2,1)}) %all-gather.13.cloned.1.call-update) | async-done | bytes 2097168 | tf_op jit(solution)/shard_map/all_gather | solution.py:150
  176.3 25.2 %while.50 = (s32[]{:T(128)}, f32[8,256]{1,0:T(8,128)S(1)}, f32[8,256]{1,0:T(8,128)S(1)}, s32[4,512]{1,0:T(4,128)S(1)}, bf16[4,8,512,64]{2,3,1,0:T(8,128)(2,1)S(1...) while((s32[]{:T(128)}, f32[8,256]{1,0:T(8,128)S(1)}, ...), condition=%wide.region_5.6_spmd.clone, body=%wide.region_2.5_spmd.clone.sunk | while | flops 142747648 | bytes 9683576 | solution.py:182
  201.5 14.8 %while.51 = (s32[]{:T(128)}, f32[8,256,64]{1,2,0:T(8,128)}, s32[4,512]{1,0:T(4,128)S(1)}, bf16[4,8,512,64]{2,3,1,0:T(8,128)(2,1)S(1)}, bf16[8,256,64]{1,2,0:T(8,...) while((s32[]{:T(128)}, f32[8,256,64]{1,2,0:T(8,128)}, ...), condition=%wide.region_7.8_spmd.clone, body=%wide.region_6.7_spmd.clone.sunk | while | flops 274071552 | bytes 2639994 | solution.py:202
  225.0 191.9 %all-gather.17.cloned.1.call-done = bf16[1024,10,1024]{2,0,1:T(8,128)(2,1)} async-done(((bf16[128,10,1024]{2,0,1:T(8,128)(2,1)}), bf16[1024,10,1024]{2,0,1:T(8,128)(2,1)}) %all-gather.17.cloned.1.call-update) | async-done | bytes 20971536 | tf_op jit(solution)/shard_map/all_gather | solution.py:219
  416.9 8.5 fusion.131
  429.8 99.0 %all-gather.19.cloned.1.call-done = bf16[1024,10,512]{2,0,1:T(8,128)(2,1)} async-done(((bf16[128,10,512]{2,0,1:T(8,128)(2,1)}), bf16[1024,10,512]{2,0,1:T(8,128)(2,1)}) %all-gather.19.cloned.1.call-update) | async-done | bytes 10485776 | tf_op jit(solution)/shard_map/all_gather | solution.py:250
  528.9 7.9 convolution_convert_fusion.4
  545.5 6.8 scatter_custom_fusion
  552.3 10.2 multiply_convert_fusion.1
  562.5 14.0 fusion.82
  576.5 8.9 gather_fusion.1
  595.1 18.4 %while.52 = (s32[]{:T(128)}, f32[8,256]{1,0:T(8,128)S(1)}, s32[4,512]{1,0:T(4,128)S(1)}, bf16[4,8,512,64]{2,3,1,0:T(8,128)(2,1)}, bf16[8,256,64]{1,2,0:T(8,128)(...) while((s32[]{:T(128)}, f32[8,256]{1,0:T(8,128)S(1)}, ...), condition=%wide.region_22.23_spmd.clone, body=%wide.region_20.22_spmd.clone.sunk | while | flops 274860032 | bytes 10273419 | solution.py:333
  613.5 44.9 %while.53 = (s32[]{:T(128)}, f32[8,256,64]{1,2,0:T(8,128)S(1)}, bf16[4,8,512,64]{2,3,1,0:T(8,128)(2,1)}, bf16[4,8,512,64]{2,3,1,0:T(8,128)(2,1)}, s32[4,512]{1,0...) while((s32[]{:T(128)}, f32[8,256,64]{1,2,0:T(8,128)S(1)}, ...), condition=%wide.region_24.25_spmd.clone, body=%wide.region_23.24_spmd.clone.sunk | while | flops 684457984 | bytes 75399968 | solution.py:361
  664.1 6.5 reshape.607
  676.4 6.5 reshape.609
  684.3 7.4 convolution_convert_fusion.1
  691.7 14.0 copy.195
  707.4 12.1 convolution_convert_fusion
  719.5 26.0 %copy.193 = bf16[1024,10240]{1,0:T(8,128)(2,1)} copy(bf16[1024,10240]{0,1:T(8,128)(2,1)} %bitcast.390) | data formatting | bytes 41943040
  749.4 63.4 %reduce-scatter.21.cloned.1.call-done = bf16[128,512]{1,0:T(8,128)(2,1)} async-done(((bf16[2048,512]{1,0:T(8,128)(2,1)}), bf16[128,512]{1,0:T(8,128)(2,1)}) %reduce-scatter.21.cloned.1.call-update) | async-done | bytes 131088
  821.9 107.0 %reduce-scatter.27.cloned.1.call-done = bf16[128,5120]{1,0:T(8,128)(2,1)} async-done(((bf16[1024,5120]{1,0:T(8,128)(2,1)}), bf16[128,5120]{1,0:T(8,128)(2,1)}) %reduce-scatter.27.cloned.1.call-update) | async-done | bytes 1310736
  931.3 209.6 %reduce-scatter.25.cloned.1.call-done = bf16[128,10240]{1,0:T(8,128)(2,1)} async-done(((bf16[1024,10240]{1,0:T(8,128)(2,1)}), bf16[128,10240]{1,0:T(8,128)(2,1)}) %reduce-scatter.25.cloned.1.call-update) | async-done | bytes 2621456
  1145.3 69.8 %reduce-scatter.17.cloned.1.call-done = bf16[128,3072]{1,0:T(8,128)(2,1)} async-done(((bf16[1024,3072]{1,0:T(8,128)(2,1)}), bf16[128,3072]{1,0:T(8,128)(2,1)}) %reduce-scatter.17.cloned.1.call-update) | async-done | bytes 786448 | tf_op jit(solution)/shard_map/reduce_scatter | solution.py:80
  1216.4 32.5 %reduce-scatter.23.cloned.1.call-done = bf16[128,10]{1,0:T(8,128)(2,1)} async-done(((bf16[1024,10]{1,0:T(8,128)(2,1)}), bf16[128,10]{1,0:T(8,128)(2,1)}) %reduce-scatter.23.cloned.1.call-update) | async-done | bytes 2576
  1253.6 13.3 all-reduce.4
  1267.1 42.3 %all-reduce.2 = (bf16[128]{0:T(256)(128)(2,1)S(1)}, bf16[128]{0:T(256)(128)(2,1)S(1)}, bf16[128,10]{0,1:T(8,128)(2,1)S(1)}) all-reduce(bf16[128]{0:T(256)(128)(2,1)S(1)} %dynamic-slice.1, bf16[128]{0:T(256)(128)(2,1)S(1)} %dynamic-slice.3, bf16[128,10]{0,1:T(8,128)(2,1)S(1)} %copy.186), channel_id=1, replica_groups=mesh['ctx'=16,'fsdp'=8] {'ctx'}, use_global_device_ids=true, to_apply=%region_30.31 | all-reduce | flops 1536 | bytes 6144 | tf_op jit(solution)/shard_map/psum | solution.py:423
  1312.1 102.8 %all-reduce.7.cloned.1.call-done = (bf16[128,3072]{1,0:T(8,128)(2,1)}, bf16[128,10,1024]{0,2,1:T(8,128)(2,1)}, bf16[128,10,512]{0,2,1:T(8,128)(2,1)}) async-done(((bf16[128,3072]{1,0:T(8,128)(2,1)}, bf16[128,10,1024]{0,2,1:T(8,128)(2,1)}, bf16[128,10,512]{0,2,1:T(8,128)(2,1)}), (bf16[128,3072]{1,0:T(8,128)(2,1)}, bf16[128,10,1024]{0,2,1:T(8,128)(2,1)}, ...) | async-done | bytes 4718608 | tf_op jit(solution)/shard_map/psum | solution.py:420
  (358 shorter events, 218.1 us)
Async XLA Ops:
  7.2 58.5 %all-gather.9.cloned.1.call-start = ((), (), s32[]{:S(2)}) async-start(), calls=%async_computation.6 | async-start | bytes 4718592 | tf_op jit(solution)/shard_map/all_gather | solution.py:125
  7.9 107.9 %all-gather.11.cloned.1.call-start = ((), (), s32[]{:S(2)}) async-start(), calls=%async_computation.7 | async-start | bytes 2228224 | tf_op jit(solution)/shard_map/all_gather | solution.py:149
  25.1 40.6 %copy-start.29 = (f32[8,1,128]{2,1,0:T(1,128)}, f32[8,1,128]{2,1,0:T(1,128)S(1)}, u32[]{:S(2)}) copy-start(f32[8,1,128]{2,1,0:T(1,128)S(1)} %convert_element_type.222) | copy-start | bytes 12292
  28.9 36.8 %copy-start.34 = (f32[128]{0:T(128)}, f32[128]{0:T(128)S(1)}, u32[]{:S(2)}) copy-start(f32[128]{0:T(128)S(1)} %add_rsqrt_fusion.1) | copy-start | bytes 1540
  29.0 78.2 %copy-start.25 = (f32[128,32]{0,1:T(8,128)}, f32[128,32]{0,1:T(8,128)S(1)}, u32[]{:S(2)}) copy-start(f32[128,32]{0,1:T(8,128)S(1)} %get-tuple-element.638) | copy-start | bytes 49156
  29.0 78.2 %copy-start.27 = (f32[128,32]{0,1:T(8,128)}, f32[128,32]{0,1:T(8,128)S(1)}, u32[]{:S(2)}) copy-start(f32[128,32]{0,1:T(8,128)S(1)} %get-tuple-element.639) | copy-start | bytes 49156
  69.0 15.4 %copy-start.31 = (s32[1,128,8]{1,2,0:T(8,128)S(1)}, s32[1,128,8]{1,2,0:T(8,128)}, u32[]{:S(2)}) copy-start(s32[1,128,8]{1,2,0:T(8,128)} %param.21) | copy-start | bytes 12292
  69.7 94.8 %all-gather.13.cloned.1.call-start = ((), (), s32[]{:S(2)}) async-start(), calls=%async_computation.8 | async-start | bytes 2228224 | tf_op jit(solution)/shard_map/all_gather | solution.py:150
  70.4 149.1 %all-gather.15.cloned.1.call-start = ((), (), s32[]{:S(2)}) async-start(), calls=%async_computation.9 | async-start | bytes 2359296 | tf_op jit(solution)/shard_map/all_gather | solution.py:126
  71.0 15.5 %copy-start.37 = (bf16[128,10]{0,1:T(8,128)(2,1)S(1)}, bf16[128,10]{0,1:T(8,128)(2,1)}, u32[]{:S(2)}) copy-start(bf16[128,10]{0,1:T(8,128)(2,1)} %param.26) | copy-start | bytes 7684
  71.0 35.1 %copy-start.24 = (bf16[1,128,1024]{2,1,0:T(8,128)(2,1)S(1)}, bf16[1,128,1024]{2,1,0:T(8,128)(2,1)}, u32[]{:S(2)}) copy-start(bf16[1,128,1024]{2,1,0:T(8,128)(2,1)} %param.29) | copy-start | bytes 786436
  71.1 345.9 %all-gather.17.cloned.1.call-start = ((), (), s32[]{:S(2)}) async-start(), calls=%async_computation.10 | async-start | bytes 23592960 | tf_op jit(solution)/shard_map/all_gather | solution.py:219
  71.6 457.2 %all-gather.19.cloned.1.call-start = ((), (), s32[]{:S(2)}) async-start(), calls=%async_computation.11 | async-start | bytes 11796480 | tf_op jit(solution)/shard_map/all_gather | solution.py:250
  72.2 676.1 %reduce-scatter.19.cloned.1.call-start = ((), (), s32[]{:S(2)}) async-start(), calls=%async_computation.13 | async-start | bytes 2228224
  201.5 18.1 %copy-start.8 = (bf16[1,128,1024]{2,1,0:T(8,128)(2,1)S(1)}, bf16[1,128,1024]{2,1,0:T(8,128)(2,1)}, u32[]{:S(2)}) copy-start(bf16[1,128,1024]{2,1,0:T(8,128)(2,1)} %param.19) | copy-start | bytes 786436
  216.3 6.0 copy-start.2
  224.9 200.5 %copy-start.3 = (bf16[1280,1024]{1,0:T(8,128)(2,1)}, bf16[1280,1024]{1,0:T(8,128)(2,1)S(1)}, u32[]{:S(2)}) copy-start(bf16[1280,1024]{1,0:T(8,128)(2,1)S(1)} %convolution_convert_fusion.2) | copy-start | bytes 7864324
  552.3 10.2 copy-start.7
  585.4 5.3 copy-start.10
  588.9 4.8 copy-start.32
  670.6 142.2 %reduce-scatter.21.cloned.1.call-start = ((), (), s32[]{:S(2)}) async-start(), calls=%async_computation.14 | async-start | bytes 2228224
  682.9 246.0 %reduce-scatter.27.cloned.1.call-start = ((), (), s32[]{:S(2)}) async-start(), calls=%async_computation.17 | async-start | bytes 11796480
  705.7 435.2 %reduce-scatter.25.cloned.1.call-start = ((), (), s32[]{:S(2)}) async-start(), calls=%async_computation.16 | async-start | bytes 23592960
  745.6 469.6 %reduce-scatter.17.cloned.1.call-start = ((), (), s32[]{:S(2)}) async-start(), calls=%async_computation.12 | async-start | bytes 7077888 | tf_op jit(solution)/shard_map/reduce_scatter | solution.py:80
  746.3 68.2 %copy-start.9 = (bf16[1,128,1024]{2,1,0:T(8,128)(2,1)S(1)}, bf16[1,128,1024]{2,1,0:T(8,128)(2,1)}, u32[]{:S(2)}) copy-start(bf16[1,128,1024]{2,1,0:T(8,128)(2,1)} %param.19) | copy-start | bytes 786436
  819.9 429.0 %reduce-scatter.23.cloned.1.call-start = ((), (), s32[]{:S(2)}) async-start(), calls=%async_computation.15 | async-start | bytes 294912
  821.9 592.9 %all-reduce.7.cloned.1.call-start = ((), (), s32[]{:S(2)}) async-start(), calls=%async_computation.18 | async-start | bytes 9437184 | tf_op jit(solution)/shard_map/psum | solution.py:420
  1145.3 69.9 %copy-start.40 = (u32[128]{0:T(128)S(1)}, u32[128]{0:T(128)}, u32[]{:S(2)}) copy-start(u32[128]{0:T(128)} %constant.145) | copy-start | bytes 1540
  1145.3 104.5 %copy-start.30 = (f32[8,1,128]{2,1,0:T(1,128)S(1)}, f32[8,1,128]{2,1,0:T(1,128)}, u32[]{:S(2)}) copy-start(f32[8,1,128]{2,1,0:T(1,128)} %copy-done.29) | copy-start | bytes 12292
  1145.3 104.5 %copy-start.35 = (f32[128]{0:T(128)S(1)}, f32[128]{0:T(128)}, u32[]{:S(2)}) copy-start(f32[128]{0:T(128)} %copy-done.34) | copy-start | bytes 1540
  1249.8 3.8 copy-start.36
  1414.8 4.1 copy-start.18
  (34 other events, 71.0 us)
Sparse Core Ops, SparseCore 0:
  9.7 56.0 all-gather.8
  69.8 45.9 all-gather.10
  118.8 45.6 all-gather.12
  166.0 34.7 all-gather.14
  202.4 214.5 all-gather.16
  418.4 110.4 all-gather.18
  670.7 67.6 reduce-scatter.18
  742.8 69.9 reduce-scatter.20
  815.2 113.6 reduce-scatter.26
  931.2 209.6 reduce-scatter.24
  1143.4 71.7 reduce-scatter.16
  1217.9 30.9 reduce-scatter.22
  1253.1 161.7 all-reduce.6
where the time goes:
time: 1440 us; the launch traced here: 1430 us
  waiting for transfers between devices  966 us (67%)
  matrix products  162 us (11%)
  local copies, waits for them, and re-layouts  138 us (10%)
  blocking collectives  104 us (7%)
  other arithmetic  43.8 us (3%)
  between operations  16.2 us (1%)
    unnamed x18, waiting for transfers between devices  415 us
    all_gather x1, waiting for transfers between devices, body(): in_piece = lax.all_gather(expert_in, 'fsdp', axis=0, tiled=True)  192 us
    psum x1, waiting for transfers between devices, body(): lax.psum(attn_rows.astype(jnp.bfloat16), 'ctx').astype(jnp.float32)  103 us
    all_gather x1, waiting for transfers between devices, body(): lax.all_gather(expert_down, 'fsdp', axis=0, tiled=True)  99 us
    unnamed x94, local copies, waits for them, and re-layouts  95.9 us
    reduce_scatter x1, waiting for transfers between devices, reduce_rows(): lax.psum_scatter(term(tuple((array for array in lefts)), rights).astype(j...  69.8 us
    psum x1, blocking collectives, body(): lax.psum(small_one.astype(jnp.bfloat16), 'ctx').astype(jnp.float32)  42.3 us
    all_gather x1, waiting for transfers between devices, body(): lax.all_gather(value_local, 'ctx', axis=0, tiled=True)  42 us
  transfers between devices with their start and end apart: 13, of which 11 were waited for; matrix products, arithmetic and copies ran while one was open for 13% of the time, Pallas kernels for 0%

commit v1 on v0

v1 whole, which is shorter than its diff:
```python
import math

import jax
import jax.numpy as jnp
from jax import lax
from jax.experimental import pallas as pl
from jax.experimental.pallas import tpu as pltpu
from jax.sharding import PartitionSpec as P

HEAD_DIM = 64
EPSILON = 1e-06
THETA = 10000.0
NEGATIVE = -1e30
BF16 = jnp.bfloat16
F32 = jnp.float32
VMEM_LIMIT = 48 * 1024 * 1024

GROUPS = [[2 * i + c for i in range(8)] for c in range(2)]
PAIRS = [(i, i ^ 1) for i in range(16)]
X_HI = [(i, i ^ 2) for i in range(16)]
X_LO = [(i, i ^ 4) for i in range(8)]
ALONG_Y = [[4 * y + i for y in range(4)] for i in range(4)]
ALONG_Z = [[4 * x + z for z in range(4)] for x in range(2)]


def exchange_ctx(parts):
    return lax.all_to_all(parts, "ctx", 0, 0, tiled=True, axis_index_groups=GROUPS)


def exchange_fsdp(parts):
    return lax.all_to_all(parts, "fsdp", 0, 0, tiled=True)


def copies(own):
    return jnp.broadcast_to(own[None], (8,) + own.shape)


def gather_ctx(own):
    return exchange_ctx(copies(own))


def gather_fsdp(own):
    return exchange_fsdp(copies(own))


def swap_core(own):
    return lax.ppermute(own, "ctx", PAIRS)


def total(parts):
    return jnp.sum(parts.astype(F32), axis=0)


def dot(left, right):
    return jnp.dot(left, right, preferred_element_type=F32)


def dot_tn(left, right):
    return lax.dot_general(left, right, (((0,), (0,)), ((), ())), preferred_element_type=F32)


def dot_nt(left, right):
    return lax.dot_general(left, right, (((1,), (1,)), ((), ())), preferred_element_type=F32)


def query_block(block, half):
    lo = 64 * half
    return jnp.concatenate([block[0:64, lo : lo + 64], block[64:128, lo : lo + 64]], axis=1)


def masked(scores, keys, position):
    rows = lax.broadcasted_iota(jnp.int32, (512, 128), 0) + (keys - 512)
    lanes = lax.broadcasted_iota(jnp.int32, (512, 128), 1) % 64 + position * 64
    tail = jnp.where(rows <= lanes, scores[keys - 512 :], NEGATIVE)
    if keys == 512:
        return tail
    return jnp.concatenate([scores[: keys - 512], tail], axis=0)


def attend_kernel(order_ref, query_ref, own_ref, other_ref, out_ref, rows_ref, cols_ref):
    for number, source_ref in enumerate((own_ref, other_ref)):
        source = source_ref[...].astype(F32).T.astype(BF16)
        for k in range(8):
            b = order_ref[number, k]
            low = pl.multiple_of(b * 64, 64)
            high = pl.multiple_of((31 - b) * 64, 64)
            rows_ref[pl.ds(low, 64), :] = source[128 * k : 128 * k + 64]
            rows_ref[pl.ds(high, 64), :] = source[128 * k + 64 : 128 * k + 128]
    cols_ref[...] = rows_ref[...].astype(F32).T.astype(BF16)
    blank = jnp.zeros((64, 128), BF16)

    def attend(block, half, position, keys):
        right = jnp.concatenate([query_block(block, half), blank], axis=0)
        scores = masked(dot(rows_ref[0:keys, :], right), keys, position)
        exponent = jnp.exp(scores - jnp.max(scores, axis=0, keepdims=True))
        share = 1.0 / jnp.sum(exponent, axis=0, keepdims=True)
        out = dot(cols_ref[64:128, 0:keys], exponent.astype(BF16)) * share
        out = out.T
        return jnp.concatenate([out[0:64], out[64:128]], axis=1).astype(BF16)

    def step(k, carry):
        start = pl.multiple_of(k * 128, 128)
        block = query_ref[:, pl.ds(start, 128)]
        b = order_ref[0, k]

        def both(low_keys, high_keys):
            out_ref[pl.ds(start, 64), :] = attend(block, 0, b, low_keys)
            out_ref[pl.ds(pl.multiple_of(start + 64, 64), 64), :] = attend(
                block, 1, 31 - b, high_keys
            )

        @pl.when(b < 8)
        def _():
            both(512, 2048)

        @pl.when(b >= 8)
        def _():
            both(1024, 1536)

        return carry

    lax.fori_loop(0, 8, step, 0)


def attend_forward(order, query, own, other):
    vmem = pl.BlockSpec(memory_space=pltpu.VMEM)
    return pl.pallas_call(
        attend_kernel,
        out_shape=(
            jax.ShapeDtypeStruct((1024, 128), BF16),
            jax.ShapeDtypeStruct((2048, 128), BF16),
            jax.ShapeDtypeStruct((128, 2048), BF16),
        ),
        in_specs=[pl.BlockSpec(memory_space=pltpu.SMEM), vmem, vmem, vmem],
        out_specs=(vmem, vmem, vmem),
        compiler_params=pltpu.CompilerParams(vmem_limit_bytes=VMEM_LIMIT),
        name="attend_forward",
        cost_estimate=cost(11),
    )(order, query, own, other)


def attend_back_kernel(
    order_ref, query_ref, rows_ref, cols_ref, branch_ref, proj_ref,
    dquery_ref, own_ref, other_ref, acc_ref, grad_ref,
):
    grad_ref[...] = dot(branch_ref[...], proj_ref[...]).astype(BF16)
    acc_ref[...] = jnp.zeros_like(acc_ref)
    blank = jnp.zeros((64, 128), BF16)
    blank_t = jnp.zeros((128, 64), BF16)

    def back(block, grads, half, position, keys):
        query = query_block(block, half)
        query_t = query.astype(F32).T.astype(BF16)
        rows = grads[64 * half : 64 * half + 64]
        grad_t = jnp.concatenate([rows[:, 0:64], rows[:, 64:128]], axis=0)
        grad = grad_t.astype(F32).T.astype(BF16)
        right = jnp.concatenate(
            [jnp.concatenate([query, blank], axis=1), jnp.concatenate([blank, grad], axis=1)],
            axis=0,
        )
        both = dot(rows_ref[0:keys, :], right)
        scores = masked(both[:, 0:128], keys, position)
        dprobs = both[:, 128:256]
        exponent = jnp.exp(scores - jnp.max(scores, axis=0, keepdims=True))
        probs = exponent * (1.0 / jnp.sum(exponent, axis=0, keepdims=True))
        weighted = probs * dprobs
        mean = jnp.sum(weighted, axis=0, keepdims=True)
        dscores = (weighted - probs * mean).astype(BF16)
        pair = jnp.concatenate([dscores, probs.astype(BF16)], axis=1)
        right_t = jnp.concatenate(
            [
                jnp.concatenate([query_t, blank_t], axis=1),
                jnp.concatenate([blank_t, grad_t], axis=1),
            ],
            axis=0,
        )
        acc_ref[0:keys, :] += dot(pair, right_t)
        return dot(cols_ref[0:64, 0:keys], dscores)

    def step(k, carry):
        start = pl.multiple_of(k * 128, 128)
        block = query_ref[:, pl.ds(start, 128)]
        grads = grad_ref[pl.ds(start, 128), :]
        b = order_ref[0, k]

        def both(low_keys, high_keys):
            low = back(block, grads, 0, b, low_keys)
            high = back(block, grads, 1, 31 - b, high_keys)
            dquery_ref[0:64, pl.ds(start, 128)] = jnp.concatenate(
                [low[:, 0:64], high[:, 0:64]], axis=1
            )
            dquery_ref[64:128, pl.ds(start, 128)] = jnp.concatenate(
                [low[:, 64:128], high[:, 64:128]], axis=1
            )

        @pl.when(b < 8)
        def _():
            both(512, 2048)

        @pl.when(b >= 8)
        def _():
            both(1024, 1536)

        return carry

    lax.fori_loop(0, 8, step, 0)
    for number, target_ref in enumerate((own_ref, other_ref)):
        for k in range(8):
            b = order_ref[number, k]
            low = acc_ref[pl.ds(pl.multiple_of(b * 64, 64), 64), :]
            high = acc_ref[pl.ds(pl.multiple_of((31 - b) * 64, 64), 64), :]
            block = jnp.concatenate([low, high], axis=0).T
            target_ref[:, 128 * k : 128 * k + 128] = block.astype(target_ref.dtype)


def attend_backward(order, query, rows, cols, branch, proj):
    vmem = pl.BlockSpec(memory_space=pltpu.VMEM)
    return pl.pallas_call(
        attend_back_kernel,
        out_shape=(
            jax.ShapeDtypeStruct((128, 1024), F32),
            jax.ShapeDtypeStruct((128, 1024), F32),
            jax.ShapeDtypeStruct((128, 1024), BF16),
        ),
        in_specs=[pl.BlockSpec(memory_space=pltpu.SMEM)] + [vmem] * 5,
        out_specs=(vmem, vmem, vmem),
        scratch_shapes=[pltpu.VMEM((2048, 128), F32), pltpu.VMEM((1024, 128), BF16)],
        compiler_params=pltpu.CompilerParams(vmem_limit_bytes=VMEM_LIMIT),
        name="attend_backward",
        cost_estimate=cost(21),
    )(order, query, rows, cols, branch, proj)


def rotate(first, second, cos_table, sin_table):
    return first * cos_table - second * sin_table, second * cos_table + first * sin_table


def cost(microseconds):
    return pl.CostEstimate(
        flops=int(microseconds * 1.1e9), bytes_accessed=int(microseconds * 3e6), transcendentals=0
    )


def vmem_spec():
    return pl.BlockSpec(memory_space=pltpu.VMEM)


def project_kernel(x_ref, weight_ref, cos_ref, sin_ref, normal_ref, query_ref, kv_ref):
    x = x_ref[...].astype(F32)
    rstd = lax.rsqrt(jnp.mean(x * x, axis=-1, keepdims=True) + EPSILON)
    normal = (x * rstd).astype(BF16)
    normal_ref[...] = normal
    mixed = dot(normal, weight_ref[...]).T
    cos_table = cos_ref[...]
    sin_table = sin_ref[...]
    scale = 1.0 / math.sqrt(HEAD_DIM)
    for h in range(3):
        low, high = rotate(
            mixed[64 * h : 64 * h + 32], mixed[64 * h + 32 : 64 * h + 64], cos_table, sin_table
        )
        turned = jnp.concatenate([low, high], axis=0).astype(BF16)
        if h < 2:
            query_ref[64 * h : 64 * h + 64] = (turned.astype(F32) * scale).astype(BF16)
        else:
            kv_ref[0:64] = turned
    kv_ref[64:128] = mixed[192:256].astype(BF16)


def project(x_all, weight, cos_table, sin_table):
    rows = pl.BlockSpec((256, 1024), lambda i: (i, 0))
    columns = pl.BlockSpec((128, 256), lambda i: (0, i))
    table = pl.BlockSpec((32, 256), lambda i: (0, i))
    return pl.pallas_call(
        project_kernel,
        grid=(4,),
        out_shape=(
            jax.ShapeDtypeStruct((1024, 1024), BF16),
            jax.ShapeDtypeStruct((128, 1024), BF16),
            jax.ShapeDtypeStruct((128, 1024), BF16),
        ),
        in_specs=[rows, pl.BlockSpec((1024, 256), lambda i: (0, 0)), table, table],
        out_specs=(rows, columns, columns),
        compiler_params=pltpu.CompilerParams(vmem_limit_bytes=VMEM_LIMIT),
        name="project",
        cost_estimate=cost(2),
    )(x_all, weight, cos_table, sin_table)


def experts_kernel(
    first_ref,
    x_ref,
    attended_ref,
    moe_ref,
    upstream_ref,
    hidden_ref,
    gates_ref,
    normal_ref,
    act_ref,
    dgate_up_ref,
    packed_ref,
):
    first = first_ref[0]
    attended = jnp.concatenate([attended_ref[j] for j in range(8)], axis=1)
    hidden = x_ref[...].astype(F32) + dot_nt(attended, moe_ref[:, 2048:3072])
    hidden_ref[...] = hidden
    rstd = lax.rsqrt(jnp.mean(hidden * hidden, axis=-1, keepdims=True) + EPSILON)
    normal = (hidden * rstd).astype(BF16)
    normal_ref[...] = normal
    lanes = lax.broadcasted_iota(jnp.int32, (256, 128), 1)
    named = upstream_ref[:, 1024:1152].astype(F32).astype(jnp.int32)
    chosen = lanes == named[:, 0:1]
    for k in range(1, 8):
        chosen = chosen | (lanes == named[:, k : k + 1])
    logits = dot(normal, moe_ref[:, 1280:1408])
    held = jnp.where(chosen, logits, NEGATIVE)
    raised = jnp.where(chosen, jnp.exp(held - jnp.max(held, axis=-1, keepdims=True)), 0.0)
    gates = raised / jnp.sum(raised, axis=-1, keepdims=True)
    gates_ref[...] = jnp.where(lanes == 64, rstd, gates)
    gate_up = dot(normal, moe_ref[:, 0:1280])
    spread = dot(upstream_ref[:, 0:1024], moe_ref[:, 1408:2048])
    dgates = jnp.zeros((256, 128), F32)
    dgate_all = []
    dup_all = []
    for c in range(5):
        gate_pre = gate_up[:, 128 * c : 128 * c + 128]
        up_pre = gate_up[:, 640 + 128 * c : 768 + 128 * c]
        back = spread[:, 128 * c : 128 * c + 128]
        weight = jnp.sum(jnp.where(lanes == first + c, gates, 0.0), axis=-1, keepdims=True)
        sigmoid = 1.0 / (1.0 + jnp.exp(-gate_pre))
        silu = gate_pre * sigmoid
        act = silu * up_pre
        act_ref[:, 128 * c : 128 * c + 128] = (weight * act).astype(BF16)
        dact = weight * back
        dgate_all.append(
            (dact * up_pre * sigmoid * (1.0 + gate_pre * (1.0 - sigmoid))).astype(BF16)
        )
        dup_all.append((dact * silu).astype(BF16))
        share = jnp.sum(act * back, axis=-1, keepdims=True)
        dgates = dgates + jnp.where((lanes % 64) == first + c, share, 0.0)
    dgate_up = jnp.concatenate(dgate_all + dup_all, axis=1)
    dgate_up_ref[...] = dgate_up
    packed_ref[:, 0:1024] = dot_nt(dgate_up, moe_ref[:, 0:1280]).astype(BF16)
    high = dgates.astype(BF16)
    low = (dgates - high.astype(F32)).astype(BF16)
    packed_ref[:, 1024:1152] = jnp.where(lanes < 64, high, low)


def experts(first, x_all, attended, moe, upstream):
    def rows(width):
        return pl.BlockSpec((256, width), lambda i: (i, 0))

    return pl.pallas_call(
        experts_kernel,
        grid=(4,),
        out_shape=(
            jax.ShapeDtypeStruct((1024, 1024), F32),
            jax.ShapeDtypeStruct((1024, 128), F32),
            jax.ShapeDtypeStruct((1024, 1024), BF16),
            jax.ShapeDtypeStruct((1024, 640), BF16),
            jax.ShapeDtypeStruct((1024, 1280), BF16),
            jax.ShapeDtypeStruct((1024, 1152), BF16),
        ),
        in_specs=[
            pl.BlockSpec(memory_space=pltpu.SMEM),
            rows(1024),
            pl.BlockSpec((8, 256, 128), lambda i: (0, i, 0)),
            pl.BlockSpec((1024, 3072), lambda i: (0, 0)),
            rows(1152),
        ],
        out_specs=(
            rows(1024),
            rows(128),
            rows(1024),
            rows(640),
            rows(1280),
            rows(1152),
        ),
        compiler_params=pltpu.CompilerParams(vmem_limit_bytes=VMEM_LIMIT),
        name="experts",
        cost_estimate=cost(16),
    )(first, x_all, attended, moe, upstream)


def middle_kernel(
    chip_ref, parts_ref, hidden_ref, gates_ref, upstream_ref, router_ref,
    dhidden_ref, dbranch_ref, dlogits_ref, normal_ref,
):
    summed = parts_ref[0].astype(F32)
    for k in range(1, 8):
        summed = summed + parts_ref[k].astype(F32)
    lanes = lax.broadcasted_iota(jnp.int32, (128, 128), 1)
    gates = jnp.where(lanes < 64, gates_ref[...], 0.0)
    rstd = gates_ref[:, 64:65]
    pair = summed[:, 1024:1152]
    dgates = jnp.where(lanes < 64, pair + pltpu.roll(pair, 64, 1), 0.0)
    dlogits = gates * (dgates - jnp.sum(gates * dgates, axis=-1, keepdims=True))
    dlogits = dlogits.astype(BF16)
    dlogits_ref[...] = dlogits
    scaled = summed[:, 0:1024] + dot_nt(dlogits, router_ref[...])
    normal = hidden_ref[...] * rstd
    normal_ref[...] = normal.astype(BF16)
    dhidden = upstream_ref[...].astype(F32) + rstd * (
        scaled - normal * jnp.mean(scaled * normal, axis=-1, keepdims=True)
    )
    dhidden_ref[...] = dhidden
    dbranch_ref[...] = dhidden.astype(BF16)


def middle(chip, parts, hidden, gates, upstream, moe):
    def own(width):
        return pl.BlockSpec((128, width), lambda i, chip: (chip[0], 0))

    def whole(*shape):
        return pl.BlockSpec(shape, lambda i, chip: (0,) * len(shape))

    return pl.pallas_call(
        middle_kernel,
        grid_spec=pltpu.PrefetchScalarGridSpec(
            num_scalar_prefetch=1,
            grid=(1,),
            in_specs=[
                whole(8, 128, 1152),
                own(1024),
                own(128),
                own(1024),
                pl.BlockSpec((1024, 128), lambda i, chip: (0, 10)),
            ],
            out_specs=(
                whole(128, 1024),
                whole(128, 1024),
                whole(128, 128),
                whole(128, 1024),
            ),
        ),
        out_shape=(
            jax.ShapeDtypeStruct((128, 1024), F32),
            jax.ShapeDtypeStruct((128, 1024), BF16),
            jax.ShapeDtypeStruct((128, 128), BF16),
            jax.ShapeDtypeStruct((128, 1024), BF16),
        ),
        compiler_params=pltpu.CompilerParams(vmem_limit_bytes=VMEM_LIMIT),
        name="middle",
        cost_estimate=cost(2),
    )(chip, parts, hidden, gates, upstream, moe)


def turn_kernel(
    query_ref, own_ref, other_ref, cos_ref, sin_ref, normal_ref, parts_ref, grad_ref
):
    kv = own_ref[...] + other_ref[...].astype(F32)
    cos_table = cos_ref[...]
    sin_table = -sin_ref[...]
    scale = 1.0 / math.sqrt(HEAD_DIM)
    turned = []
    for source in (query_ref[0:64] * scale, query_ref[64:128] * scale, kv[0:64]):
        turned += list(rotate(source[0:32], source[32:64], cos_table, sin_table))
    mixed = jnp.concatenate(turned + [kv[64:128]], axis=0).astype(BF16)
    for k in range(8):
        parts_ref[k] = mixed[:, 128 * k : 128 * k + 128]
    grad_ref[...] = dot(mixed, normal_ref[...]).T.astype(BF16)


def turn(query, own, other, cos_table, sin_table, normal):
    return pl.pallas_call(
        turn_kernel,
        out_shape=(
            jax.ShapeDtypeStruct((8, 256, 128), BF16),
            jax.ShapeDtypeStruct((1024, 256), BF16),
        ),
        in_specs=[vmem_spec()] * 6,
        out_specs=(vmem_spec(), vmem_spec()),
        compiler_params=pltpu.CompilerParams(vmem_limit_bytes=VMEM_LIMIT),
        name="turn",
        cost_estimate=cost(2),
    )(query, own, other, cos_table, sin_table, normal)


def finish_kernel(dmixed_ref, weight_ref, dhidden_ref, x_ref, out_ref):
    dmixed = dmixed_ref[...].astype(F32).T.astype(BF16)
    scaled = dot_nt(dmixed, weight_ref[...])
    x = x_ref[...].astype(F32)
    rstd = lax.rsqrt(jnp.mean(x * x, axis=-1, keepdims=True) + EPSILON)
    normal = x * rstd
    out_ref[...] = dhidden_ref[...] + rstd * (
        scaled - normal * jnp.mean(scaled * normal, axis=-1, keepdims=True)
    )


def finish(dmixed, weight, dhidden, x_own):
    return pl.pallas_call(
        finish_kernel,
        out_shape=jax.ShapeDtypeStruct((128, 1024), F32),
        in_specs=[vmem_spec()] * 4,
        out_specs=vmem_spec(),
        compiler_params=pltpu.CompilerParams(vmem_limit_bytes=VMEM_LIMIT),
        name="finish",
        cost_estimate=cost(2),
    )(dmixed, weight, dhidden, x_own)


def spread_kernel(
    core_ref, own_gate, own_up, own_down, other_gate, other_up, other_down,
    weight_ref, gain_ref, in_ref, down_ref, sums_ref,
):
    @pl.when(pl.program_id(0) == 0)
    def _():
        sums_ref[...] = jnp.zeros_like(sums_ref)

    def write(sources, row):
        gate, up, down = sources
        gain = gain_ref[row : row + 64]
        place = slice(row, row + 64)
        for q in range(4):
            near = 128 * (q + (1 - 2 * (q % 2)) * core_ref[1])
            for source, start in ((gate, 0), (up, 512)):
                lanes = pl.ds(pl.multiple_of(start + near, 128), 128)
                raw = source[q].astype(F32)
                in_ref[0, place, lanes] = raw * gain
                sums_ref[place] += raw * weight_ref[0, place, lanes].astype(F32)
            down_ref[0, place, pl.ds(pl.multiple_of(near, 128), 128)] = down[q].astype(F32)

    own = (own_gate, own_up, own_down)
    other = (other_gate, other_up, other_down)

    @pl.when(core_ref[0] == 0)
    def _():
        write(own, 0)
        write(other, 64)

    @pl.when(core_ref[0] == 1)
    def _():
        write(other, 0)
        write(own, 64)


def spread_experts(core, own, other, weight, gain):
    def piece(start):
        return pl.BlockSpec((4, 64, 128), lambda e: (e // 5, 0, start + e % 5))

    pieces = [piece(0), piece(5), piece(10)]
    return pl.pallas_call(
        spread_kernel,
        grid=(10,),
        out_shape=(
            jax.ShapeDtypeStruct((10, 128, 1024), F32),
            jax.ShapeDtypeStruct((10, 128, 512), F32),
            jax.ShapeDtypeStruct((128, 128), F32),
        ),
        in_specs=[pl.BlockSpec(memory_space=pltpu.SMEM)]
        + pieces
        + pieces
        + [
            pl.BlockSpec((1, 128, 1024), lambda e: (e, 0, 0)),
            pl.BlockSpec((128, 1), lambda e: (0, 0)),
        ],
        out_specs=(
            pl.BlockSpec((1, 128, 1024), lambda e: (e, 0, 0)),
            pl.BlockSpec((1, 128, 512), lambda e: (e, 0, 0)),
            pl.BlockSpec((128, 128), lambda e: (0, 0)),
        ),
        compiler_params=pltpu.CompilerParams(vmem_limit_bytes=VMEM_LIMIT),
        name="spread_experts",
        cost_estimate=cost(9),
    )(core, own, own, own, other, other, other, weight, gain)


def spread_attention_kernel(
    core_ref, own_ref, other_ref, weight_ref, gain_ref, qkv_ref, proj_ref, router_ref, sums_ref
):
    def write(source_ref, row):
        gain = gain_ref[row : row + 64]
        place = slice(row, row + 64)
        raw = [source_ref[j].astype(F32) for j in range(8)]
        query = jnp.concatenate([part[:, 0:128] for part in raw], axis=1)
        key = jnp.concatenate([part[:, 128:192] for part in raw], axis=1)
        value = jnp.concatenate([part[:, 192:256] for part in raw], axis=1)
        qkv = jnp.concatenate([query, key, value], axis=1)
        qkv_ref[place] = qkv * gain
        sums_ref[place] = jnp.sum(qkv * weight_ref[place].astype(F32), axis=-1, keepdims=True)
        router = raw[0][:, 384:512]
        for j in range(8):
            proj_ref[place, 128 * j : 128 * j + 128] = raw[j][:, 256:384]
            if j > 0:
                router = router + raw[j][:, 384:512]
        router_ref[place] = router

    @pl.when(core_ref[0] == 0)
    def _():
        write(own_ref, 0)
        write(other_ref, 64)

    @pl.when(core_ref[0] == 1)
    def _():
        write(other_ref, 0)
        write(own_ref, 64)


def spread_attention(core, own, other, weight, gain):
    return pl.pallas_call(
        spread_attention_kernel,
        out_shape=(
            jax.ShapeDtypeStruct((128, 2048), F32),
            jax.ShapeDtypeStruct((128, 1024), F32),
            jax.ShapeDtypeStruct((128, 128), F32),
            jax.ShapeDtypeStruct((128, 1), F32),
        ),
        in_specs=[pl.BlockSpec(memory_space=pltpu.SMEM)] + [vmem_spec()] * 4,
        out_specs=tuple([vmem_spec()] * 4),
        compiler_params=pltpu.CompilerParams(vmem_limit_bytes=VMEM_LIMIT),
        name="spread_attention",
        cost_estimate=cost(2),
    )(core, own, other, weight, gain)


def fold_cores(core, parts):
    split = parts.reshape(8, 2, 64, parts.shape[2])
    mine = jnp.where(core == 0, split[:, 0], split[:, 1])
    theirs = jnp.where(core == 0, split[:, 1], split[:, 0])
    return (mine.astype(F32) + swap_core(theirs).astype(F32)).astype(BF16)


def gather_weights(pair):
    return lax.all_gather(pair, "fsdp", axis=0, tiled=False, axis_index_groups=ALONG_Z)


def join_weights(core, x_lo, gathered):
    other = swap_core(gathered)
    low = jnp.where(core == 0, gathered, other)
    high = jnp.where(core == 0, other, gathered)
    joined = jnp.stack([low, high], axis=2)
    first = jnp.where(x_lo == 0, joined[:, 0], joined[:, 1])
    second = jnp.where(x_lo == 0, joined[:, 1], joined[:, 0])
    return jnp.stack([first, second]).reshape(1024, gathered.shape[3])


def scatter_experts(x_lo, parts):
    split = parts.reshape(2, 4, 64, parts.shape[2])
    mine = jnp.where(x_lo == 0, split[0], split[1])
    theirs = jnp.where(x_lo == 0, split[1], split[0])
    return lax.psum_scatter(
        jnp.stack([mine, theirs], axis=1).reshape(512, parts.shape[2]),
        "fsdp",
        scatter_dimension=0,
        tiled=True,
        axis_index_groups=ALONG_Z,
    )


def body(
    tokens,
    block_order,
    routes,
    attn_gain,
    qkv_weight,
    proj_weight,
    moe_gain,
    router_weight,
    expert_in,
    expert_down,
    cotangent,
):
    index = lax.axis_index("ctx")
    chip = index // 2
    core = index % 2
    x_hi = chip % 2
    x_lo = lax.axis_index("fsdp") // 4
    x_own = tokens.reshape(128, 1024)
    g_own = cotangent.reshape(128, 1024)
    gain_one = attn_gain.astype(F32)[:, None]
    gain_two = moe_gain.astype(F32)[:, None]

    qkv_turned = jnp.concatenate(
        [
            qkv_weight[:, 0:1024].reshape(128, 8, 128),
            qkv_weight[:, 1024:1536].reshape(128, 8, 64),
            qkv_weight[:, 1536:2048].reshape(128, 8, 64),
        ],
        axis=2,
    ).reshape(128, 2048)
    qkv_turned = (qkv_turned.astype(F32) * gain_one).astype(BF16)
    qkv_part = lax.dynamic_slice(qkv_turned, (0, 256 * chip), (128, 256))
    qkv_slice = gather_fsdp(qkv_part).reshape(1024, 256)

    proj_half = lax.dynamic_slice(proj_weight, (64 * core, 0), (64, 1024))
    first = 5 * (chip // 4)
    lane = 128 * (chip % 4)
    in_by_expert = expert_in.transpose(1, 0, 2)
    down_by_expert = expert_down.transpose(1, 0, 2)
    row = 64 * core

    def piece(source, offset):
        taken = lax.dynamic_slice(source, (first, row, offset + lane), (5, 64, 128))
        return taken.transpose(1, 0, 2).reshape(64, 640)

    router_half = lax.dynamic_slice(router_weight, (row, 0), (64, 10))
    gain_half = lax.dynamic_slice(gain_two, (row, 0), (64, 1))
    with_gain = jnp.concatenate(
        [piece(in_by_expert, 0), piece(in_by_expert, 512)]
        + [jnp.pad(router_half, ((0, 0), (0, 118)))],
        axis=1,
    )
    with_gain = (with_gain.astype(F32) * gain_half).astype(BF16)
    moe_half = jnp.concatenate([with_gain, piece(down_by_expert, 0), proj_half], axis=1)
    moe_other = lax.ppermute(moe_half, "fsdp", X_LO)
    qkv_half = lax.dynamic_slice(qkv_turned, (row, 0), (64, 2048))
    qkv_other = lax.ppermute(qkv_half, "fsdp", X_LO)
    qkv_slice, moe_pieces, x_copies = lax.optimization_barrier(
        (qkv_slice, jnp.stack([moe_half, moe_other]), copies(x_own))
    )
    moe_gathered = gather_weights(moe_pieces)
    x_all = exchange_ctx(x_copies).reshape(1024, 1024)

    routes_low = jnp.pad(routes.reshape(128, 8).astype(BF16), ((0, 0), (0, 120)))
    g_copies = copies(jnp.concatenate([g_own, routes_low], axis=1))
    x_all, g_copies = lax.optimization_barrier((x_all, g_copies))
    upstream = exchange_ctx(g_copies).reshape(1024, 1152)

    orders = block_order.reshape(8, 2)
    order_own = jnp.where(core == 0, orders[:, 0], orders[:, 1])
    order_other = jnp.where(core == 0, orders[:, 1], orders[:, 0])
    order = jnp.stack([order_own, order_other])
    within = jnp.arange(128, dtype=jnp.int32)
    placed = jnp.where(within[None, :] < 64, order_own[:, None], 31 - order_own[:, None])
    positions = (placed * 64 + within[None, :] % 64).reshape(1, 1024)
    frequency = THETA ** (-(jnp.arange(32, dtype=F32) * 2.0) / HEAD_DIM)
    angles = frequency[:, None] * positions.astype(F32)
    cos_table = jnp.cos(angles)
    sin_table = jnp.sin(angles)

    xh_one, query, key_value = project(
        x_all,
        qkv_slice,
        cos_table,
        sin_table,
    )
    attended, kv_rows, kv_cols = attend_forward(order, query, key_value, swap_core(key_value))

    attended, upstream, moe_gathered, qkv_pieces = lax.optimization_barrier(
        (attended, upstream, moe_gathered, jnp.stack([qkv_half, qkv_other]))
    )
    moe_full = join_weights(core, x_lo, moe_gathered)
    qkv_gathered = gather_weights(qkv_pieces)

    hidden, gates, xh_two, act_gated, dgate_up, packed = experts(
        first.reshape(1).astype(jnp.int32),
        x_all,
        gather_ctx(attended),
        moe_full,
        upstream,
    )
    packed, qkv_gathered = lax.optimization_barrier((packed, qkv_gathered))
    parts = exchange_ctx(packed.reshape(8, 128, 1152))

    down_slice = moe_full[:, 1408:2048]
    out_part = dot_nt(act_gated, down_slice).astype(BF16)
    in_grad = dot_tn(xh_two, dgate_up).astype(BF16)
    down_grad = dot_tn(upstream[:, 0:1024], act_gated).astype(BF16)
    moe_fold = fold_cores(
        core, jnp.concatenate([in_grad, down_grad], axis=1).reshape(8, 128, 1920)
    )
    proj_slice = lax.dynamic_slice(moe_full, (0, 2048 + 128 * chip), (1024, 128))
    parts, out_part, moe_fold, proj_slice = lax.optimization_barrier(
        (parts, out_part, moe_fold, proj_slice)
    )
    moe_sum = scatter_experts(x_lo, moe_fold).reshape(2, 64, 1920)
    moe_near = lax.ppermute(moe_sum[1], "fsdp", X_LO)

    own_rows = 128 * chip
    hidden_own = lax.dynamic_slice(hidden, (own_rows, 0), (128, 1024))
    dhidden, dbranch, dlogits, normal_two = middle(
        chip.reshape(1).astype(jnp.int32), parts, hidden, gates, upstream, moe_full
    )
    dbranch_all = gather_ctx(dbranch).reshape(1024, 1024)
    qkv_full = join_weights(core, x_lo, qkv_gathered)
    dbranch_all, out_part, qkv_full, moe_near = lax.optimization_barrier(
        (dbranch_all, out_part, qkv_full, moe_near)
    )
    moe_sum = (moe_sum[0].astype(F32) + moe_near.astype(F32)).astype(BF16)
    moe_pair = jnp.stack([moe_sum, lax.ppermute(moe_sum, "ctx", X_HI)])
    out_parts = exchange_ctx(out_part.reshape(8, 128, 1024))
    router_part = dot_tn(normal_two, dlogits).astype(BF16)
    proj_part = dot_tn(dbranch_all, attended).astype(BF16)

    dquery, dkv_own, dkv_other = attend_backward(
        order, query, kv_rows, kv_cols, dbranch_all, proj_slice
    )
    dkv_other, out_parts, moe_pair = lax.optimization_barrier((dkv_other, out_parts, moe_pair))
    moe_own = lax.all_gather(moe_pair, "ctx", axis=0, tiled=True, axis_index_groups=ALONG_Y)
    layer_out = (hidden_own + total(out_parts)).astype(BF16)
    dmixed, qkv_part_grad = turn(
        dquery, dkv_own, swap_core(dkv_other), cos_table, sin_table, xh_one
    )
    attn_fold = fold_cores(
        core,
        jnp.concatenate([qkv_part_grad, proj_part, router_part], axis=1).reshape(8, 128, 512),
    )
    attn_parts, moe_own = lax.optimization_barrier((exchange_fsdp(attn_fold), moe_own))
    attn_sum = total(attn_parts).astype(BF16).reshape(1, 256, 128)
    tail = exchange_ctx(
        jnp.concatenate([dmixed, jnp.broadcast_to(attn_sum, (8, 256, 128))], axis=1)
    )
    in_grad, down_grad, gain_sums = spread_experts(
        jnp.stack([core, x_hi]).astype(jnp.int32),
        moe_own,
        swap_core(moe_own),
        in_by_expert,
        gain_two,
    )
    tail, in_grad, down_grad, gain_sums = lax.optimization_barrier(
        (tail, in_grad, down_grad, gain_sums)
    )
    dmixed_own = tail[:, 0:256].reshape(2048, 128)
    attn_own = tail[:, 256:512].reshape(8, 64, 512)
    tokens_grad = finish(dmixed_own, qkv_full, dhidden, x_own)
    qkv_grad, proj_grad, router_raw, attn_gain_grad = spread_attention(
        core.reshape(1).astype(jnp.int32), attn_own, swap_core(attn_own), qkv_weight, gain_one
    )
    router_raw = router_raw[:, 0:10]
    attn_gain_grad = attn_gain_grad.reshape(128)
    expert_in_grad = in_grad.transpose(1, 0, 2)
    expert_down_grad = down_grad.transpose(1, 0, 2)
    router_grad = router_raw * gain_two
    moe_gain_grad = jnp.sum(gain_sums, axis=1) + jnp.sum(
        router_raw * router_weight.astype(F32), axis=1
    )
    return (
        layer_out.reshape(1, 128, 1024),
        tokens_grad.reshape(1, 128, 1024),
        attn_gain_grad,
        qkv_grad,
        proj_grad,
        moe_gain_grad,
        router_grad,
        expert_in_grad,
        expert_down_grad,
    )


def solution(mesh):
    in_specs = (
        P("fsdp", "ctx", None),
        P(),
        P("fsdp", "ctx", None),
        P("fsdp"),
        P("fsdp", None),
        P("fsdp", None),
        P("fsdp"),
        P("fsdp", None),
        P("fsdp", None, None),
        P("fsdp", None, None),
        P("fsdp", "ctx", None),
    )
    out_specs = (
        P("fsdp", "ctx", None),
        P("fsdp", "ctx", None),
        P("fsdp"),
        P("fsdp", None),
        P("fsdp", None),
        P("fsdp"),
        P("fsdp", None),
        P("fsdp", None, None),
        P("fsdp", None, None),
    )
    return jax.shard_map(body, mesh=mesh, in_specs=in_specs, out_specs=out_specs, check_vma=False)
```

time: 1440 us -> 357 us (0.25)
  waiting for transfers between devices: 966 us -> 110 us
  matrix products: 162 us -> 13.1 us
  local copies, waits for them, and re-layouts: 138 us -> 41.3 us
  blocking collectives: 104 us -> 11.6 us
  Pallas kernels: 0 us -> 66.3 us
  starting transfers between devices: 0.52 us -> 62.6 us
    unnamed x18 -> x4, waiting for transfers between devices: 415 us -> 0.57 us
    all_gather x6 -> x3, waiting for transfers between devices: 378 us -> 13.1 us  [the longest x1 13.1 us: body(): lax.all_gather(moe_pair, 'ctx', axis=0, tiled=True, axis_index_groups=ALO...]
    dot_general x54 -> x5, matrix products: 162 us -> 13.1 us  [the longest x4 8.15 us: dot_tn(): lax.dot_general(left, right, (((0,), (0,)), ((), ())), preferred_element_...]
    psum x1 -> x0, waiting for transfers between devices: 103 us -> none  [body(): lax.psum(attn_rows.astype(jnp.bfloat16), 'ctx').astype(jnp.float32)]
    all_to_all x0 -> x8, waiting for transfers between devices: none -> 83.6 us  [the longest x7 77.2 us: exchange_ctx(): lax.all_to_all(parts, 'ctx', 0, 0, tiled=True, axis_index_groups=GROUPS)]
    unnamed x94 -> x91, local copies, waits for them, and re-layouts: 95.9 us -> 19.4 us
    pallas_call x0 -> x9, Pallas kernels: none -> 66.3 us  [the longest x1 21.1 us: attend_backward(): pl.pallas_call(attend_back_kernel, out_shape=(jax.ShapeDtypeStruct((128,...]
    reduce_scatter x1, waiting for transfers between devices: 69.8 us -> 9.24 us  [scatter_experts(): lax.psum_scatter(jnp.stack([mine, theirs], axis=1).reshape(512, parts.sha...]
  transfers between devices with their start and end apart: 13 -> 24, of which waited for: 11 -> 13; matrix products, arithmetic and copies ran while one was open for 13% -> 18% of each run, Pallas kernels for 0% -> 18%
where the time goes in v1:
time: 357 us; the launch traced here: 356 us
  waiting for transfers between devices  110 us (31%)
  Pallas kernels  66.3 us (19%)
  starting transfers between devices  62.6 us (18%)
  local copies, waits for them, and re-layouts  41.3 us (12%)
  other arithmetic  36.2 us (10%)
  between operations  14.6 us (4%)
  matrix products  13.1 us (4%)
  blocking collectives  11.6 us (3%)
    all_to_all x7, waiting for transfers between devices, exchange_ctx(): lax.all_to_all(parts, 'ctx', 0, 0, tiled=True, axis_index_groups=GROUPS)  77.2 us
    all_to_all x7, starting transfers between devices, exchange_ctx(): lax.all_to_all(parts, 'ctx', 0, 0, tiled=True, axis_index_groups=GROUPS)  33 us
    pallas_call x1, Pallas kernels, attend_backward(): pl.pallas_call(attend_back_kernel, out_shape=(jax.ShapeDtypeStruct((128,...  21.1 us
    unnamed x91, local copies, waits for them, and re-layouts  19.4 us
    ppermute x8, starting transfers between devices, swap_core(): return lax.ppermute(own, 'ctx', PAIRS)  16.9 us
    pallas_call x1, Pallas kernels, experts(): pl.pallas_call(experts_kernel, grid=(4,), out_shape=(jax.ShapeDtypeStruct...  16.4 us
    all_gather x1, waiting for transfers between devices, body(): lax.all_gather(moe_pair, 'ctx', axis=0, tiled=True, axis_index_groups=ALO...  13.1 us
    all_to_all x1, blocking collectives, exchange_fsdp(): return lax.all_to_all(parts, 'fsdp', 0, 0, tiled=True)  11.6 us
  transfers between devices with their start and end apart: 24, of which 13 were waited for; matrix products, arithmetic and copies ran while one was open for 18% of the time, Pallas kernels for 18%

profile of v1, /device:TPU:1, one launch (start us, length us, event | category | flops | bytes accessed | tf_op | source)
XLA Modules:
  0.0 355.9 jit_solution(15732337298517114207)
XLA Ops:
  14.8 5.0 %all-to-all-start = ((bf16[8,128,256]{2,1,0:T(8,128)(2,1)}), bf16[8,128,256]{2,1,0:T(8,128)(2,1)S(1)}, u32[]{:S(2)}, u32[]{:S(2)}) async-start(bf16[8,128,256]{2,1,0:T(8,128)(2,1)} %broadcast_in_dim.77), calls=%async_computation | async-start | bytes 1048576 | tf_op jit(solution)/shard_map/all_to_all | solution.py:31
  22.8 6.4 %all-to-all-done = bf16[8,128,256]{2,1,0:T(8,128)(2,1)S(1)} async-done(((bf16[8,128,256]{2,1,0:T(8,128)(2,1)}), bf16[8,128,256]{2,1,0:T(8,128)(2,1)S(1)}, u32[]{:S(2)}, u32[]{:S(2)}) %all-to-all-start) | async-done | bytes 524320 | tf_op jit(solution)/shard_map/all_to_all | solution.py:31
  30.8 6.6 %all-to-all-start.1 = ((bf16[8,128,1024]{2,1,0:T(8,128)(2,1)}), bf16[8,128,1024]{2,1,0:T(8,128)(2,1)S(1)}, u32[]{:S(2)}, u32[]{:S(2)}) async-start(bf16[8,128,1024]{2,1,0:T(8,128)(2,1)} %broadcast_in_dim.79), calls=%async_computation.1 | async-start | bytes 4194304 | tf_op jit(solution)/shard_map/all_to_all | solution.py:27
  40.3 23.3 %all-to-all-done.1 = bf16[8,128,1024]{2,1,0:T(8,128)(2,1)S(1)} async-done(((bf16[8,128,1024]{2,1,0:T(8,128)(2,1)}), bf16[8,128,1024]{2,1,0:T(8,128)(2,1)S(1)}, u32[]{:S(2)}, u32[]{:S(2)}) %all-to-all-start.1) | async-done | bytes 2097184 | tf_op jit(solution)/shard_map/all_to_all | solution.py:27
  65.3 5.2 %all-to-all-start.2 = ((bf16[8,128,1152]{2,1,0:T(8,128)(2,1)}), bf16[8,128,1152]{2,1,0:T(8,128)(2,1)}, u32[]{:S(2)}, u32[]{:S(2)}) async-start(bf16[8,128,1152]{2,1,0:T(8,128)(2,1)} %broadcast_in_dim.80), calls=%async_computation.2 | async-start | bytes 4718592 | tf_op jit(solution)/shard_map/all_to_all | solution.py:27
  75.2 5.2 %collective-permute-start.1 = (bf16[128,1024]{1,0:T(8,128)(2,1)S(1)}, bf16[128,1024]{1,0:T(8,128)(2,1)S(1)}, u32[]{:S(2)}, u32[]{:S(2)}) collective-permute-start(bf16[128,1024]{1,0:T(8,128)(2,1)S(1)} %get-tuple-element.69.own_ref), channel_id=1, source_target_pairs={{0,8},{8,0},{16,24},{24,16},{32,40},{40,32},{48,56},{56,48},{64,72... | collective-permute-start | bytes 786440 | tf_op jit(solution)/shard_map/ppermute | solution.py:47
  83.3 10.7 %attend_forward.1 = (bf16[1024,128]{1,0:T(8,128)(2,1)S(1)}, bf16[2048,128]{1,0:T(8,128)(2,1)S(1)}, bf16[128,2048]{1,0:T(8,128)(2,1)S(1)}) custom-call(s32[2,8]{1,0:T(2,128)S(1)} %pad_add_fusion.order_ref, bf16[128,1024]{1,0:T(8,128)(2,1)S(1)} %copy-done.25, bf16[128,1024]{1,0:T(8,128)(2,1)S(1)} %get-tuple-element.69.own_ref, ...), custom_call_target="tpu_custom_call" | custom-call | flops 12099999744 | bytes 33000000 | tf_op jit(solution)/shard_map/attend_forward/pallas_call | solution.py:127
  96.7 6.2 %collective-permute-start.3 = (bf16[4,2,64,3072]{3,2,1,0:T(8,128)(2,1)}, bf16[4,2,64,3072]{3,2,1,0:T(8,128)(2,1)}, u32[]{:S(2)}, u32[]{:S(2)}) collective-permute-start(bf16[4,2,64,3072]{3,2,1,0:T(8,128)(2,1)} %bitcast.180), channel_id=1, source_target_pairs={{0,8},{8,0},{16,24},{24,16},{32,40},{40,32},{48,56},{56,48},{64,72... | collective-permute-start | bytes 9437192 | tf_op jit(solution)/shard_map/ppermute | solution.py:47
  104.4 4.4 %all-to-all-start.3 = ((bf16[8,1024,128]{2,1,0:T(8,128)(2,1)}), bf16[8,1024,128]{2,1,0:T(8,128)(2,1)}, u32[]{:S(2)}, u32[]{:S(2)}) async-start(bf16[8,1024,128]{2,1,0:T(8,128)(2,1)} %broadcast_in_dim.86), calls=%async_computation.3 | async-start | bytes 4194304 | tf_op jit(solution)/shard_map/all_to_all | solution.py:27
  109.6 3.3 select_bitcast_fusion.1
  114.6 3.1 copy.84
  117.7 19.7 %all-to-all-done.3.attended_ref = bf16[8,1024,128]{2,1,0:T(8,128)(2,1)} async-done(((bf16[8,1024,128]{2,1,0:T(8,128)(2,1)}), bf16[8,1024,128]{2,1,0:T(8,128)(2,1)}, u32[]{:S(2)}, u32[]{:S(2)}) %all-to-all-start.3) | async-done | bytes 2097184 | tf_op jit(solution)/shard_map/all_to_all | solution.py:27
  137.4 16.4 %experts.1 = (f32[1024,1024]{1,0:T(8,128)}, f32[1024,128]{1,0:T(8,128)S(1)}, bf16[1024,1024]{1,0:T(8,128)(2,1)S(1)}, bf16[1024,640]{1,0:T(8,128)(2,1)S(1)}, bf16...) custom-call(s32[1]{0:T(128)} %bitcast.first_ref, bf16[1024,1024]{1,0:T(8,128)(2,1)S(1)} %bitcast.164, ...), custom_call_target="tpu_custom_call" | custom-call | flops 17600000000 | bytes 48000000 | tf_op jit(solution)/shard_map/experts/pallas_call | solution.py:352
  153.9 4.0 %fusion.11 = bf16[1024,640]{1,0:T(8,128)(2,1)S(1)} fusion(bf16[1024,640]{1,0:T(8,128)(2,1)S(1)} %get-tuple-element.82, bf16[1024,1152]{1,0:T(8,128)(2,1)} %bitcast.11.upstream_ref), kind=kOutput, calls=%fused_computation.35 | convolution fusion | flops 1342832640 | bytes 4718592 | tf_op jit(solution)/shard_map/dot_general | solution.py:59
  157.8 3.2 convolution_convert_fusion
  164.7 3.6 %all-to-all-start.4 = ((bf16[8,128,1152]{2,1,0:T(8,128)(2,1)}), bf16[8,128,1152]{2,1,0:T(8,128)(2,1)S(1)}, u32[]{:S(2)}, u32[]{:S(2)}) async-start(bf16[8,128,1152]{2,1,0:T(8,128)(2,1)} %bitcast.182), calls=%async_computation.4 | async-start | bytes 4718592 | tf_op jit(solution)/shard_map/all_to_all | solution.py:27
  170.1 5.0 %convolution_convert_fusion.1 = bf16[1024,1024]{1,0:T(8,128)(2,1)} fusion(bf16[1024,640]{1,0:T(8,128)(2,1)} %copy-done.19, bf16[1024,3072]{1,0:T(8,128)(2,1)} %bitcast.173), kind=kOutput, calls=%fused_computation.34 | convolution fusion | flops 1343225856 | bytes 4718592 | tf_op jit(solution)/shard_map/dot_general | solution.py:63
  175.1 3.6 %fusion = bf16[8,64,1920]{2,1,0:T(8,128)(2,1)} fusion(bf16[8,64,1920]{2,1,0:T(8,128)(2,1)} %collective-permute-done.4, pred[]{:T(512)S(6)} %eq.10, bf16[8,2,64,1920]{3,2,1,0:T(8,128)(2,1)S(1)} %bitcast.170), kind=kLoop, calls=%fused_computation.11 | loop fusion | flops 4915200 | bytes 7864321 | tf_op jit(solution)/shard_map/convert_element_type | solution.py:619
  178.7 21.0 %all-to-all-done.4.parts_ref = bf16[8,128,1152]{2,1,0:T(8,128)(2,1)S(1)} async-done(((bf16[8,128,1152]{2,1,0:T(8,128)(2,1)}), bf16[8,128,1152]{2,1,0:T(8,128)(2,1)S(1)}, u32[]{:S(2)}, u32[]{:S(2)}) %all-to-all-start.4) | async-done | bytes 2359328 | tf_op jit(solution)/shard_map/all_to_all | solution.py:27
  209.8 3.6 %all-to-all-start.5 = ((bf16[8,128,1024]{2,1,0:T(8,128)(2,1)}), bf16[8,128,1024]{2,1,0:T(8,128)(2,1)S(1)}, u32[]{:S(2)}, u32[]{:S(2)}) async-start(bf16[8,128,1024]{2,1,0:T(8,128)(2,1)} %broadcast_in_dim.87), calls=%async_computation.5 | async-start | bytes 4194304 | tf_op jit(solution)/shard_map/all_to_all | solution.py:27
  213.4 2.5 select_bitcast_fusion.3
  219.1 9.2 %reduce-scatter.2.cloned.1.call-done = bf16[128,1920]{1,0:T(8,128)(2,1)} async-done(((bf16[512,1920]{1,0:T(8,128)(2,1)}), bf16[128,1920]{1,0:T(8,128)(2,1)}) %reduce-scatter.2.cloned.1.call-update) | async-done | bytes 491536 | tf_op jit(solution)/shard_map/reduce_scatter | solution.py:640
  231.2 2.6 pad_maximum_fusion.1
  236.1 5.8 %all-to-all-done.5 = bf16[8,128,1024]{2,1,0:T(8,128)(2,1)S(1)} async-done(((bf16[8,128,1024]{2,1,0:T(8,128)(2,1)}), bf16[8,128,1024]{2,1,0:T(8,128)(2,1)S(1)}, u32[]{:S(2)}, u32[]{:S(2)}) %all-to-all-start.5) | async-done | bytes 2097184 | tf_op jit(solution)/shard_map/all_to_all | solution.py:27
  243.3 4.0 %collective-permute-start.7 = (bf16[64,1920]{1,0:T(8,128)(2,1)}, bf16[64,1920]{1,0:T(8,128)(2,1)}, u32[]{:S(2)}, u32[]{:S(2)}) collective-permute-start(bf16[64,1920]{1,0:T(8,128)(2,1)} %add_convert_fusion.1), channel_id=1, source_target_pairs={{0,16},{8,24},{16,0},{24,8},{32,48},{40,56},{48,32},{56,40},{64,80... | collective-permute-start | bytes 737288 | tf_op jit(solution)/shard_map/ppermute | solution.py:779
  247.3 4.5 %all-to-all-start.6 = ((bf16[8,128,1024]{2,1,0:T(8,128)(2,1)}), bf16[8,128,1024]{2,1,0:T(8,128)(2,1)}, u32[]{:S(2)}, u32[]{:S(2)}) async-start(bf16[8,128,1024]{2,1,0:T(8,128)(2,1)} %bitcast.183), calls=%async_computation.7 | async-start | bytes 4194304 | tf_op jit(solution)/shard_map/all_to_all | solution.py:27
  254.9 21.1 %attend_backward.1 = (f32[128,1024]{1,0:T(8,128)S(1)}, f32[128,1024]{1,0:T(8,128)S(1)}, bf16[128,1024]{1,0:T(8,128)(2,1)S(1)}) custom-call(s32[2,8]{1,0:T(2,128)S(1)} %pad_add_fusion.order_ref, bf16[128,1024]{1,0:T(8,128)(2,1)S(1)} %copy-done.26, bf16[2048,128]{1,0:T(8,128)(2,1)S(1)} %copy-done.28, bf16[128,2048]{1,0:T(8,128)(2,1)S(1)} %copy-done.30, ...), custom_call_target="tpu_custom_call" | custom-call | flops 23100000256 | bytes 63000000 | tf_op jit(solution)/shard_map/attend_backward/pallas_call | solution.py:218
  286.4 11.6 %all_to_all.45 = bf16[8,64,512]{2,1,0:T(8,128)(2,1)S(1)} all-to-all(bf16[8,64,512]{2,1,0:T(8,128)(2,1)S(1)} %fusion.15), channel_id=1, replica_groups=mesh['ctx'=16,'fsdp'=8] {'fsdp'}, dimensions={0} | all-to-all | bytes 1048576 | tf_op jit(solution)/shard_map/all_to_all | solution.py:31
  298.0 13.1 %all-gather.6.cloned.1.call-done.own_gate.own_up.own_down = bf16[8,64,1920]{2,1,0:T(8,128)(2,1)} async-done(((bf16[2,64,1920]{2,1,0:T(8,128)(2,1)}), bf16[8,64,1920]{2,1,0:T(8,128)(2,1)}) %all-gather.6.cloned.1.call-update) | async-done | bytes 1966096 | tf_op jit(solution)/shard_map/all_gather | solution.py:788
  313.5 5.1 %all-to-all-start.8 = ((bf16[8,512,128]{2,1,0:T(8,128)(2,1)}), bf16[8,512,128]{2,1,0:T(8,128)(2,1)S(1)}, u32[]{:S(2)}, u32[]{:S(2)}) async-start(bf16[8,512,128]{2,1,0:T(8,128)(2,1)} %pad_maximum_fusion.7), calls=%async_computation.9 | async-start | bytes 2097152 | tf_op jit(solution)/shard_map/all_to_all | solution.py:27
  320.1 9.3 %spread_experts.1 = (f32[10,128,1024]{2,1,0:T(8,128)}, f32[10,128,512]{2,1,0:T(8,128)}, f32[128,128]{1,0:T(8,128)S(1)}) custom-call(s32[2]{0:T(128)S(1)} %pad_add_fusion.1.core_ref, bf16[8,64,1920]{2,1,0:T(8,128)(2,1)S(1)} %copy-done.13, bf16[8,64,1920]{2,1,0:T(8,128)(2,1)S(1)} %copy-done.13, bf16[8,64,1920]{2,1,0:T(8,128)(2,1)S(1)} %copy-done.13, ...), custom_call_target="tpu_custom_call" | custom-call | flops 9900000256 | bytes 27000000 | tf_op jit(solution)/shard_map/spread_experts/pallas_call | solution.py:541
  329.5 6.2 %all-to-all-done.8 = bf16[8,512,128]{2,1,0:T(8,128)(2,1)S(1)} async-done(((bf16[8,512,128]{2,1,0:T(8,128)(2,1)}), bf16[8,512,128]{2,1,0:T(8,128)(2,1)S(1)}, u32[]{:S(2)}, u32[]{:S(2)}) %all-to-all-start.8) | async-done | bytes 1048608 | tf_op jit(solution)/shard_map/all_to_all | solution.py:27
  (200 shorter events, 86.6 us)
Async XLA Ops:
  10.2 10.6 %collective-permute-start = (bf16[64,3072]{1,0:T(8,128)(2,1)S(1)}, bf16[64,3072]{1,0:T(8,128)(2,1)}, u32[]{:S(2)}, u32[]{:S(2)}) collective-permute-start(bf16[64,3072]{1,0:T(8,128)(2,1)S(1)} %get-tuple-element.164), channel_id=1, source_target_pairs={{0,4},{1,5},{2,6},{3,7},{4,0},{5,1},{6,2},{7,3},{8,12},{9,13},{10,... | collective-permute-start | bytes 1179656 | tf_op jit(solution)/shard_map/ppermute | solution.py:704
  13.8 15.4 %copy-start.5 = (bf16[1,128,1024]{2,1,0:T(8,128)(2,1)S(1)}, bf16[1,128,1024]{2,1,0:T(8,128)(2,1)}, u32[]{:S(2)}) copy-start(bf16[1,128,1024]{2,1,0:T(8,128)(2,1)} %param.11) | copy-start | bytes 786436
  14.8 14.4 %all-to-all-start = ((bf16[8,128,256]{2,1,0:T(8,128)(2,1)}), bf16[8,128,256]{2,1,0:T(8,128)(2,1)S(1)}, u32[]{:S(2)}, u32[]{:S(2)}) async-start(bf16[8,128,256]{2,1,0:T(8,128)(2,1)} %broadcast_in_dim.77), calls=%async_computation | async-start | bytes 1048576 | tf_op jit(solution)/shard_map/all_to_all | solution.py:31
  19.8 76.9 %all-gather.8.cloned.1.call-start = ((), (), s32[]{:S(2)}) async-start(), calls=%async_computation.12 | async-start | bytes 3932160 | tf_op jit(solution)/shard_map/all_gather | solution.py:623
  30.8 7.5 %copy-start.37 = (s32[16]{0:T(128)S(1)}, s32[16]{0:T(128)}, u32[]{:S(2)}) copy-start(s32[16]{0:T(128)} %param.12) | copy-start | bytes 196
  30.8 32.8 %all-to-all-start.1 = ((bf16[8,128,1024]{2,1,0:T(8,128)(2,1)}), bf16[8,128,1024]{2,1,0:T(8,128)(2,1)S(1)}, u32[]{:S(2)}, u32[]{:S(2)}) async-start(bf16[8,128,1024]{2,1,0:T(8,128)(2,1)} %broadcast_in_dim.79), calls=%async_computation.1 | async-start | bytes 4194304 | tf_op jit(solution)/shard_map/all_to_all | solution.py:27
  38.1 42.3 %collective-permute-start.2 = (bf16[64,2048]{1,0:T(8,128)(2,1)}, bf16[64,2048]{1,0:T(8,128)(2,1)}, u32[]{:S(2)}, u32[]{:S(2)}) collective-permute-start(bf16[64,2048]{1,0:T(8,128)(2,1)} %constant_dynamic-slice_fusion.1), channel_id=1, source_target_pairs={{0,4},{1,5},{2,6},{3,7},{4,0},{5,1},{6,2},{7,3},{8,12},{9,13},{10,... | collective-permute-start | bytes 786440 | tf_op jit(solution)/shard_map/ppermute | solution.py:706
  65.3 31.3 %all-to-all-start.2 = ((bf16[8,128,1152]{2,1,0:T(8,128)(2,1)}), bf16[8,128,1152]{2,1,0:T(8,128)(2,1)}, u32[]{:S(2)}, u32[]{:S(2)}) async-start(bf16[8,128,1152]{2,1,0:T(8,128)(2,1)} %broadcast_in_dim.80), calls=%async_computation.2 | async-start | bytes 4718592 | tf_op jit(solution)/shard_map/all_to_all | solution.py:27
  71.1 9.3 %copy-start.33 = (bf16[1,64,2048]{2,1,0:T(8,128)(2,1)S(1)}, bf16[1,64,2048]{2,1,0:T(8,128)(2,1)}, u32[]{:S(2)}) copy-start(bf16[1,64,2048]{2,1,0:T(8,128)(2,1)} %fusion.36) | copy-start | bytes 786436
  75.2 7.1 %collective-permute-start.1 = (bf16[128,1024]{1,0:T(8,128)(2,1)S(1)}, bf16[128,1024]{1,0:T(8,128)(2,1)S(1)}, u32[]{:S(2)}, u32[]{:S(2)}) collective-permute-start(bf16[128,1024]{1,0:T(8,128)(2,1)S(1)} %get-tuple-element.69.own_ref), channel_id=1, source_target_pairs={{0,8},{8,0},{16,24},{24,16},{32,40},{40,32},{48,56},{56,48},{64,72... | collective-permute-start | bytes 786440 | tf_op jit(solution)/shard_map/ppermute | solution.py:47
  96.7 12.9 %collective-permute-start.3 = (bf16[4,2,64,3072]{3,2,1,0:T(8,128)(2,1)}, bf16[4,2,64,3072]{3,2,1,0:T(8,128)(2,1)}, u32[]{:S(2)}, u32[]{:S(2)}) collective-permute-start(bf16[4,2,64,3072]{3,2,1,0:T(8,128)(2,1)} %bitcast.180), channel_id=1, source_target_pairs={{0,8},{8,0},{16,24},{24,16},{32,40},{40,32},{48,56},{56,48},{64,72... | collective-permute-start | bytes 9437192 | tf_op jit(solution)/shard_map/ppermute | solution.py:47
  104.4 33.0 %all-to-all-start.3 = ((bf16[8,1024,128]{2,1,0:T(8,128)(2,1)}), bf16[8,1024,128]{2,1,0:T(8,128)(2,1)}, u32[]{:S(2)}, u32[]{:S(2)}) async-start(bf16[8,1024,128]{2,1,0:T(8,128)(2,1)} %broadcast_in_dim.86), calls=%async_computation.3 | async-start | bytes 4194304 | tf_op jit(solution)/shard_map/all_to_all | solution.py:27
  108.8 55.9 %all-gather.10.cloned.1.call-start = ((), (), s32[]{:S(2)}) async-start(), calls=%async_computation.13 | async-start | bytes 2621440 | tf_op jit(solution)/shard_map/all_gather | solution.py:623
  163.9 11.2 %collective-permute-start.4 = (bf16[8,64,1920]{2,1,0:T(8,128)(2,1)}, bf16[8,64,1920]{2,1,0:T(8,128)(2,1)}, u32[]{:S(2)}, u32[]{:S(2)}) collective-permute-start(bf16[8,64,1920]{2,1,0:T(8,128)(2,1)} %fusion.9), channel_id=1, source_target_pairs={{0,8},{8,0},{16,24},{24,16},{32,40},{40,32},{48,56},{56,48},{64,72... | collective-permute-start | bytes 5898248 | tf_op jit(solution)/shard_map/ppermute | solution.py:47
  164.7 35.0 %all-to-all-start.4 = ((bf16[8,128,1152]{2,1,0:T(8,128)(2,1)}), bf16[8,128,1152]{2,1,0:T(8,128)(2,1)S(1)}, u32[]{:S(2)}, u32[]{:S(2)}) async-start(bf16[8,128,1152]{2,1,0:T(8,128)(2,1)} %bitcast.182), calls=%async_computation.4 | async-start | bytes 4718592 | tf_op jit(solution)/shard_map/all_to_all | solution.py:27
  168.4 60.0 %reduce-scatter.2.cloned.1.call-start = ((), (), s32[]{:S(2)}) async-start(), calls=%async_computation.10 | async-start | bytes 2457600 | tf_op jit(solution)/shard_map/reduce_scatter | solution.py:640
  203.1 10.3 %collective-permute-start.5 = (bf16[4,2,64,2048]{3,2,1,0:T(8,128)(2,1)}, bf16[4,2,64,2048]{3,2,1,0:T(8,128)(2,1)}, u32[]{:S(2)}, u32[]{:S(2)}) collective-permute-start(bf16[4,2,64,2048]{3,2,1,0:T(8,128)(2,1)} %bitcast.184), channel_id=1, source_target_pairs={{0,8},{8,0},{16,24},{24,16},{32,40},{40,32},{48,56},{56,48},{64,72... | collective-permute-start | bytes 6291464 | tf_op jit(solution)/shard_map/ppermute | solution.py:47
  209.8 32.1 %all-to-all-start.5 = ((bf16[8,128,1024]{2,1,0:T(8,128)(2,1)}), bf16[8,128,1024]{2,1,0:T(8,128)(2,1)S(1)}, u32[]{:S(2)}, u32[]{:S(2)}) async-start(bf16[8,128,1024]{2,1,0:T(8,128)(2,1)} %broadcast_in_dim.87), calls=%async_computation.5 | async-start | bytes 4194304 | tf_op jit(solution)/shard_map/all_to_all | solution.py:27
  230.0 12.5 %collective-permute-start.6 = (bf16[64,1920]{1,0:T(8,128)(2,1)}, bf16[64,1920]{1,0:T(8,128)(2,1)S(1)}, u32[]{:S(2)}, u32[]{:S(2)}) collective-permute-start(bf16[64,1920]{1,0:T(8,128)(2,1)} %slice.111), channel_id=1, source_target_pairs={{0,4},{1,5},{2,6},{3,7},{4,0},{5,1},{6,2},{7,3},{8,12},{9,13},{10,... | collective-permute-start | bytes 737288 | tf_op jit(solution)/shard_map/ppermute | solution.py:766
  233.8 8.7 %copy-start.34 = (bf16[128,1920]{1,0:T(8,128)(2,1)S(1)}, bf16[128,1920]{1,0:T(8,128)(2,1)}, u32[]{:S(2)}) copy-start(bf16[128,1920]{1,0:T(8,128)(2,1)} %reduce-scatter.2.cloned.1.call-done) | copy-start | bytes 1474564
  243.3 35.1 %collective-permute-start.7 = (bf16[64,1920]{1,0:T(8,128)(2,1)}, bf16[64,1920]{1,0:T(8,128)(2,1)}, u32[]{:S(2)}, u32[]{:S(2)}) collective-permute-start(bf16[64,1920]{1,0:T(8,128)(2,1)} %add_convert_fusion.1), channel_id=1, source_target_pairs={{0,16},{8,24},{16,0},{24,8},{32,48},{40,56},{48,32},{56,40},{64,80... | collective-permute-start | bytes 737288 | tf_op jit(solution)/shard_map/ppermute | solution.py:779
  247.3 32.9 %all-to-all-start.6 = ((bf16[8,128,1024]{2,1,0:T(8,128)(2,1)}), bf16[8,128,1024]{2,1,0:T(8,128)(2,1)}, u32[]{:S(2)}, u32[]{:S(2)}) async-start(bf16[8,128,1024]{2,1,0:T(8,128)(2,1)} %bitcast.183), calls=%async_computation.7 | async-start | bytes 4194304 | tf_op jit(solution)/shard_map/all_to_all | solution.py:27
  251.8 59.2 %all-gather.6.cloned.1.call-start = ((), (), s32[]{:S(2)}) async-start(), calls=%async_computation.11 | async-start | bytes 2457600 | tf_op jit(solution)/shard_map/all_gather | solution.py:788
  254.9 25.4 %copy-start.8 = (bf16[128,1024]{1,0:T(8,128)(2,1)S(1)}, bf16[128,1024]{1,0:T(8,128)(2,1)}, u32[]{:S(2)}) copy-start(bf16[128,1024]{1,0:T(8,128)(2,1)} %copy-done.7) | copy-start | bytes 786436
  254.9 25.4 %copy-start.12 = (bf16[128,128]{1,0:T(8,128)(2,1)S(1)}, bf16[128,128]{1,0:T(8,128)(2,1)}, u32[]{:S(2)}) copy-start(bf16[128,128]{1,0:T(8,128)(2,1)} %copy-done.11) | copy-start | bytes 98308
  280.6 2.5 collective-permute-start.8
  284.1 27.7 %copy-start.35 = (bf16[128,10]{0,1:T(8,128)(2,1)S(1)}, bf16[128,10]{0,1:T(8,128)(2,1)}, u32[]{:S(2)}) copy-start(bf16[128,10]{0,1:T(8,128)(2,1)} %param.18) | copy-start | bytes 7684
  284.1 27.8 %copy-start.39 = (bf16[128]{0:T(256)(128)(2,1)S(1)}, bf16[128]{0:T(256)(128)(2,1)}, u32[]{:S(2)}) copy-start(bf16[128]{0:T(256)(128)(2,1)} %param.17) | copy-start | bytes 772
  284.2 2.0 collective-permute-start.9
  311.1 7.5 %collective-permute-start.10 = (bf16[8,64,1920]{2,1,0:T(8,128)(2,1)}, bf16[8,64,1920]{2,1,0:T(8,128)(2,1)}, u32[]{:S(2)}, u32[]{:S(2)}) collective-permute-start(bf16[8,64,1920]{2,1,0:T(8,128)(2,1)} %all-gather.6.cloned.1.call-done.own_gate.own_up.own_down), channel_id=1, source_target_pairs={{0,8},{8,0},{16,24},{24,16},{32,40},{40,32},{48,56},{56,48},{64,72... | collective-permute-start | bytes 5898248 | tf_op jit(solution)/shard_map/ppermute | solution.py:47
  313.5 22.2 %all-to-all-start.8 = ((bf16[8,512,128]{2,1,0:T(8,128)(2,1)}), bf16[8,512,128]{2,1,0:T(8,128)(2,1)S(1)}, u32[]{:S(2)}, u32[]{:S(2)}) async-start(bf16[8,512,128]{2,1,0:T(8,128)(2,1)} %pad_maximum_fusion.7), calls=%async_computation.9 | async-start | bytes 2097152 | tf_op jit(solution)/shard_map/all_to_all | solution.py:27
  336.1 9.8 %collective-permute-start.11 = (bf16[8,64,512]{2,1,0:T(8,128)(2,1)S(1)}, bf16[8,64,512]{2,1,0:T(8,128)(2,1)S(1)}, u32[]{:S(2)}, u32[]{:S(2)}) collective-permute-start(bf16[8,64,512]{2,1,0:T(8,128)(2,1)S(1)} %reshape.325.own_ref), channel_id=1, source_target_pairs={{0,8},{8,0},{16,24},{24,16},{32,40},{40,32},{48,56},{56,48},{64,72... | collective-permute-start | bytes 1572872 | tf_op jit(solution)/shard_map/ppermute | solution.py:47
  (33 other events, 78.5 us)
Sparse Core Ops, SparseCore 0:
  30.9 40.6 all-gather.7
  111.3 30.7 all-gather.9
  203.2 25.0 reduce-scatter.1
  280.4 30.6 all-gather.5

commit v2 on v1

--- a/solution.py
+++ b/solution.py
@@ -498,70 +498,61 @@
     )(dmixed, weight, dhidden, x_own)
 
 
-def spread_kernel(
-    core_ref, own_gate, own_up, own_down, other_gate, other_up, other_down,
-    weight_ref, gain_ref, in_ref, down_ref, sums_ref,
-):
+def spread_kernel(place_ref, gate_ref, up_ref, down_ref, weight_ref, gain_ref, *refs):
+    out_in_ref, out_down_ref, sums_ref = refs[-3:]
+
     @pl.when(pl.program_id(0) == 0)
     def _():
         sums_ref[...] = jnp.zeros_like(sums_ref)
 
-    def write(sources, row):
-        gate, up, down = sources
-        gain = gain_ref[row : row + 64]
-        place = slice(row, row + 64)
-        for q in range(4):
-            near = 128 * (q + (1 - 2 * (q % 2)) * core_ref[1])
-            for source, start in ((gate, 0), (up, 512)):
-                lanes = pl.ds(pl.multiple_of(start + near, 128), 128)
-                raw = source[q].astype(F32)
-                in_ref[0, place, lanes] = raw * gain
-                sums_ref[place] += raw * weight_ref[0, place, lanes].astype(F32)
-            down_ref[0, place, pl.ds(pl.multiple_of(near, 128), 128)] = down[q].astype(F32)
-
-    own = (own_gate, own_up, own_down)
-    other = (other_gate, other_up, other_down)
-
-    @pl.when(core_ref[0] == 0)
-    def _():
-        write(own, 0)
-        write(other, 64)
-
-    @pl.when(core_ref[0] == 1)
-    def _():
-        write(other, 0)
-        write(own, 64)
-
-
-def spread_experts(core, own, other, weight, gain):
+    gain = gain_ref[...]
+    for q in range(4):
+        near = 128 * (q + (1 - 2 * (q % 2)) * place_ref[1])
+        for source_ref, start in ((gate_ref, 0), (up_ref, 512)):
+            lanes = pl.ds(pl.multiple_of(start + near, 128), 128)
+            raw = source_ref[q].astype(F32)
+            out_in_ref[0, :, lanes] = raw * gain
+            sums_ref[...] += raw * weight_ref[0, :, lanes].astype(F32)
+        lanes = pl.ds(pl.multiple_of(near, 128), 128)
+        out_down_ref[0, :, lanes] = down_ref[q].astype(F32)
+
+
+def spread_experts(place, source, weight, gain, filled=()):
     def piece(start):
-        return pl.BlockSpec((4, 64, 128), lambda e: (e // 5, 0, start + e % 5))
-
-    pieces = [piece(0), piece(5), piece(10)]
+        return pl.BlockSpec((4, 64, 128), lambda e, place: (e // 5, 0, start + e % 5))
+
+    def rows(width):
+        return pl.BlockSpec((1, 64, width), lambda e, place: (e, place[0], 0))
+
     return pl.pallas_call(
         spread_kernel,
-        grid=(10,),
+        grid_spec=pltpu.PrefetchScalarGridSpec(
+            num_scalar_prefetch=1,
+            grid=(10,),
+            in_specs=[
+                piece(0),
+                piece(5),
+                piece(10),
+                rows(1024),
+                pl.BlockSpec((64, 1), lambda e, place: (place[0], 0)),
+            ]
+            + [pl.BlockSpec(memory_space=pl.ANY)] * len(filled),
+            out_specs=(
+                rows(1024),
+                rows(512),
+                pl.BlockSpec((64, 128), lambda e, place: (place[0], 0)),
+            ),
+        ),
         out_shape=(
             jax.ShapeDtypeStruct((10, 128, 1024), F32),
             jax.ShapeDtypeStruct((10, 128, 512), F32),
             jax.ShapeDtypeStruct((128, 128), F32),
         ),
-        in_specs=[pl.BlockSpec(memory_space=pltpu.SMEM)]
-        + pieces
-        + pieces
-        + [
-            pl.BlockSpec((1, 128, 1024), lambda e: (e, 0, 0)),
-            pl.BlockSpec((128, 1), lambda e: (0, 0)),
-        ],
-        out_specs=(
-            pl.BlockSpec((1, 128, 1024), lambda e: (e, 0, 0)),
-            pl.BlockSpec((1, 128, 512), lambda e: (e, 0, 0)),
-            pl.BlockSpec((128, 128), lambda e: (0, 0)),
-        ),
+        input_output_aliases={6 + i: i for i in range(len(filled))},
         compiler_params=pltpu.CompilerParams(vmem_limit_bytes=VMEM_LIMIT),
         name="spread_experts",
-        cost_estimate=cost(9),
-    )(core, own, own, own, other, other, other, weight, gain)
+        cost_estimate=cost(5),
+    )(place, source, source, source, weight, gain, *filled)
 
 
 def spread_attention_kernel(
@@ -794,21 +785,15 @@
         core,
         jnp.concatenate([qkv_part_grad, proj_part, router_part], axis=1).reshape(8, 128, 512),
     )
-    attn_parts, moe_own = lax.optimization_barrier((exchange_fsdp(attn_fold), moe_own))
+    attn_parts, layer_out = lax.optimization_barrier((exchange_fsdp(attn_fold), layer_out))
     attn_sum = total(attn_parts).astype(BF16).reshape(1, 256, 128)
     tail = exchange_ctx(
         jnp.concatenate([dmixed, jnp.broadcast_to(attn_sum, (8, 256, 128))], axis=1)
     )
-    in_grad, down_grad, gain_sums = spread_experts(
-        jnp.stack([core, x_hi]).astype(jnp.int32),
-        moe_own,
-        swap_core(moe_own),
-        in_by_expert,
-        gain_two,
-    )
-    tail, in_grad, down_grad, gain_sums = lax.optimization_barrier(
-        (tail, in_grad, down_grad, gain_sums)
-    )
+    own_place = jnp.stack([core, x_hi]).astype(jnp.int32)
+    other_place = jnp.stack([1 - core, x_hi]).astype(jnp.int32)
+    filled = spread_experts(own_place, moe_own, in_by_expert, gain_two)
+    tail, *filled = lax.optimization_barrier((tail, *filled))
     dmixed_own = tail[:, 0:256].reshape(2048, 128)
     attn_own = tail[:, 256:512].reshape(8, 64, 512)
     tokens_grad = finish(dmixed_own, qkv_full, dhidden, x_own)
@@ -817,6 +802,9 @@
     )
     router_raw = router_raw[:, 0:10]
     attn_gain_grad = attn_gain_grad.reshape(128)
+    in_grad, down_grad, gain_sums = spread_experts(
+        other_place, swap_core(moe_own), in_by_expert, gain_two, tuple(filled)
+    )
     expert_in_grad = in_grad.transpose(1, 0, 2)
     expert_down_grad = down_grad.transpose(1, 0, 2)
     router_grad = router_raw * gain_two

time: 357 us -> 354 us (level)
  blocking collectives: 11.6 us -> 0 us
  waiting for transfers between devices: 110 us -> 101 us
  starting transfers between devices: 62.6 us -> 69.5 us
  local copies, waits for them, and re-layouts: 41.3 us -> 46.6 us
    all_to_all x1 -> x0, blocking collectives: 11.6 us -> none  [exchange_fsdp(): return lax.all_to_all(parts, 'fsdp', 0, 0, tiled=True)]
    all_gather x1, waiting for transfers between devices: 13.1 us -> 4.18 us  [body(): lax.all_gather(moe_pair, 'ctx', axis=0, tiled=True, axis_index_groups=ALO...]
    all_to_all x7, waiting for transfers between devices: 77.2 us -> 72.2 us  [exchange_ctx(): lax.all_to_all(parts, 'ctx', 0, 0, tiled=True, axis_index_groups=GROUPS)]
    all_to_all x1 -> x2, waiting for transfers between devices: 6.4 us -> 10.9 us  [exchange_fsdp(): return lax.all_to_all(parts, 'fsdp', 0, 0, tiled=True)]
    all_to_all x1 -> x2, starting transfers between devices: 5.03 us -> 8.53 us  [exchange_fsdp(): return lax.all_to_all(parts, 'fsdp', 0, 0, tiled=True)]
    unnamed x91 -> x95, local copies, waits for them, and re-layouts: 19.4 us -> 22.9 us
    pallas_call x1 -> x2, Pallas kernels: 9.31 us -> 12.7 us  [spread_experts(): pl.pallas_call(spread_kernel, grid_spec=pltpu.PrefetchScalarGridSpec(num_...]
  transfers between devices with their start and end apart: 24 -> 25, of which waited for: 13 -> 14; matrix products, arithmetic and copies ran while one was open for 18% -> 19% of each run, Pallas kernels for 18% -> 18%
where the time goes in v2:
time: 354 us; the launch traced here: 352 us
  waiting for transfers between devices  101 us (29%)
  Pallas kernels  69.7 us (20%)
  starting transfers between devices  69.5 us (20%)
  local copies, waits for them, and re-layouts  46.6 us (13%)
  other arithmetic  37.1 us (10%)
  between operations  14.5 us (4%)
  matrix products  13.2 us (4%)
    all_to_all x7, waiting for transfers between devices, exchange_ctx(): lax.all_to_all(parts, 'ctx', 0, 0, tiled=True, axis_index_groups=GROUPS)  72.2 us
    all_to_all x7, starting transfers between devices, exchange_ctx(): lax.all_to_all(parts, 'ctx', 0, 0, tiled=True, axis_index_groups=GROUPS)  34.3 us
    unnamed x95, local copies, waits for them, and re-layouts  22.9 us
    pallas_call x1, Pallas kernels, attend_backward(): pl.pallas_call(attend_back_kernel, out_shape=(jax.ShapeDtypeStruct((128,...  21.2 us
    ppermute x8, starting transfers between devices, swap_core(): return lax.ppermute(own, 'ctx', PAIRS)  19 us
    pallas_call x1, Pallas kernels, experts(): pl.pallas_call(experts_kernel, grid=(4,), out_shape=(jax.ShapeDtypeStruct...  16.4 us
    pallas_call x2, Pallas kernels, spread_experts(): pl.pallas_call(spread_kernel, grid_spec=pltpu.PrefetchScalarGridSpec(num_...  12.7 us
    all_to_all x2, waiting for transfers between devices, exchange_fsdp(): return lax.all_to_all(parts, 'fsdp', 0, 0, tiled=True)  10.9 us
  transfers between devices with their start and end apart: 25, of which 14 were waited for; matrix products, arithmetic and copies ran while one was open for 19% of the time, Pallas kernels for 18%

profile of v2, /device:TPU:1, one launch (start us, length us, event | category | flops | bytes accessed | tf_op | source)
XLA Modules:
  0.0 351.6 jit_solution(9686449112112046856)
XLA Ops:
  14.8 5.0 %all-to-all-start = ((bf16[8,128,256]{2,1,0:T(8,128)(2,1)}), bf16[8,128,256]{2,1,0:T(8,128)(2,1)S(1)}, u32[]{:S(2)}, u32[]{:S(2)}) async-start(bf16[8,128,256]{2,1,0:T(8,128)(2,1)} %broadcast_in_dim.77), calls=%async_computation | async-start | bytes 1048576 | tf_op jit(solution)/shard_map/all_to_all | solution.py:31
  22.8 6.4 %all-to-all-done = bf16[8,128,256]{2,1,0:T(8,128)(2,1)S(1)} async-done(((bf16[8,128,256]{2,1,0:T(8,128)(2,1)}), bf16[8,128,256]{2,1,0:T(8,128)(2,1)S(1)}, u32[]{:S(2)}, u32[]{:S(2)}) %all-to-all-start) | async-done | bytes 524320 | tf_op jit(solution)/shard_map/all_to_all | solution.py:31
  30.8 6.6 %all-to-all-start.1 = ((bf16[8,128,1024]{2,1,0:T(8,128)(2,1)}), bf16[8,128,1024]{2,1,0:T(8,128)(2,1)S(1)}, u32[]{:S(2)}, u32[]{:S(2)}) async-start(bf16[8,128,1024]{2,1,0:T(8,128)(2,1)} %broadcast_in_dim.79), calls=%async_computation.1 | async-start | bytes 4194304 | tf_op jit(solution)/shard_map/all_to_all | solution.py:27
  40.3 23.3 %all-to-all-done.1 = bf16[8,128,1024]{2,1,0:T(8,128)(2,1)S(1)} async-done(((bf16[8,128,1024]{2,1,0:T(8,128)(2,1)}), bf16[8,128,1024]{2,1,0:T(8,128)(2,1)S(1)}, u32[]{:S(2)}, u32[]{:S(2)}) %all-to-all-start.1) | async-done | bytes 2097184 | tf_op jit(solution)/shard_map/all_to_all | solution.py:27
  65.3 5.2 %all-to-all-start.2 = ((bf16[8,128,1152]{2,1,0:T(8,128)(2,1)}), bf16[8,128,1152]{2,1,0:T(8,128)(2,1)}, u32[]{:S(2)}, u32[]{:S(2)}) async-start(bf16[8,128,1152]{2,1,0:T(8,128)(2,1)} %broadcast_in_dim.80), calls=%async_computation.2 | async-start | bytes 4718592 | tf_op jit(solution)/shard_map/all_to_all | solution.py:27
  75.2 5.2 %collective-permute-start.1 = (bf16[128,1024]{1,0:T(8,128)(2,1)S(1)}, bf16[128,1024]{1,0:T(8,128)(2,1)S(1)}, u32[]{:S(2)}, u32[]{:S(2)}) collective-permute-start(bf16[128,1024]{1,0:T(8,128)(2,1)S(1)} %get-tuple-element.72.own_ref), channel_id=1, source_target_pairs={{0,8},{8,0},{16,24},{24,16},{32,40},{40,32},{48,56},{56,48},{64,72... | collective-permute-start | bytes 786440 | tf_op jit(solution)/shard_map/ppermute | solution.py:47
  83.3 10.7 %attend_forward.1 = (bf16[1024,128]{1,0:T(8,128)(2,1)S(1)}, bf16[2048,128]{1,0:T(8,128)(2,1)S(1)}, bf16[128,2048]{1,0:T(8,128)(2,1)S(1)}) custom-call(s32[2,8]{1,0:T(2,128)S(1)} %pad_add_fusion.order_ref, bf16[128,1024]{1,0:T(8,128)(2,1)S(1)} %copy-done.27, bf16[128,1024]{1,0:T(8,128)(2,1)S(1)} %get-tuple-element.72.own_ref, ...), custom_call_target="tpu_custom_call" | custom-call | flops 12099999744 | bytes 33000000 | tf_op jit(solution)/shard_map/attend_forward/pallas_call | solution.py:127
  96.7 6.2 %collective-permute-start.3 = (bf16[4,2,64,3072]{3,2,1,0:T(8,128)(2,1)}, bf16[4,2,64,3072]{3,2,1,0:T(8,128)(2,1)}, u32[]{:S(2)}, u32[]{:S(2)}) collective-permute-start(bf16[4,2,64,3072]{3,2,1,0:T(8,128)(2,1)} %bitcast.182), channel_id=1, source_target_pairs={{0,8},{8,0},{16,24},{24,16},{32,40},{40,32},{48,56},{56,48},{64,72... | collective-permute-start | bytes 9437192 | tf_op jit(solution)/shard_map/ppermute | solution.py:47
  104.4 4.3 %all-to-all-start.3 = ((bf16[8,1024,128]{2,1,0:T(8,128)(2,1)}), bf16[8,1024,128]{2,1,0:T(8,128)(2,1)}, u32[]{:S(2)}, u32[]{:S(2)}) async-start(bf16[8,1024,128]{2,1,0:T(8,128)(2,1)} %broadcast_in_dim.86), calls=%async_computation.3 | async-start | bytes 4194304 | tf_op jit(solution)/shard_map/all_to_all | solution.py:27
  109.5 3.3 select_bitcast_fusion.1
  114.6 3.1 copy.89
  117.7 19.7 %all-to-all-done.3.attended_ref = bf16[8,1024,128]{2,1,0:T(8,128)(2,1)} async-done(((bf16[8,1024,128]{2,1,0:T(8,128)(2,1)}), bf16[8,1024,128]{2,1,0:T(8,128)(2,1)}, u32[]{:S(2)}, u32[]{:S(2)}) %all-to-all-start.3) | async-done | bytes 2097184 | tf_op jit(solution)/shard_map/all_to_all | solution.py:27
  137.4 16.4 %experts.1 = (f32[1024,1024]{1,0:T(8,128)}, f32[1024,128]{1,0:T(8,128)S(1)}, bf16[1024,1024]{1,0:T(8,128)(2,1)S(1)}, bf16[1024,640]{1,0:T(8,128)(2,1)S(1)}, bf16...) custom-call(s32[1]{0:T(128)} %bitcast.11.first_ref, bf16[1024,1024]{1,0:T(8,128)(2,1)S(1)} %bitcast.164, ...), custom_call_target="tpu_custom_call" | custom-call | flops 17600000000 | bytes 48000000 | tf_op jit(solution)/shard_map/experts/pallas_call | solution.py:352
  153.8 3.9 %fusion.11 = bf16[1024,640]{1,0:T(8,128)(2,1)S(1)} fusion(bf16[1024,640]{1,0:T(8,128)(2,1)S(1)} %get-tuple-element.84, bf16[1024,1152]{1,0:T(8,128)(2,1)} %bitcast.12.upstream_ref), kind=kOutput, calls=%fused_computation.35 | convolution fusion | flops 1342832640 | bytes 4718592 | tf_op jit(solution)/shard_map/dot_general | solution.py:59
  157.8 3.2 convolution_convert_fusion
  164.7 3.6 %all-to-all-start.4 = ((bf16[8,128,1152]{2,1,0:T(8,128)(2,1)}), bf16[8,128,1152]{2,1,0:T(8,128)(2,1)S(1)}, u32[]{:S(2)}, u32[]{:S(2)}) async-start(bf16[8,128,1152]{2,1,0:T(8,128)(2,1)} %bitcast.184), calls=%async_computation.4 | async-start | bytes 4718592 | tf_op jit(solution)/shard_map/all_to_all | solution.py:27
  170.1 5.0 %convolution_convert_fusion.1 = bf16[1024,1024]{1,0:T(8,128)(2,1)} fusion(bf16[1024,640]{1,0:T(8,128)(2,1)} %copy-done.21, bf16[1024,3072]{1,0:T(8,128)(2,1)} %bitcast.175), kind=kOutput, calls=%fused_computation.34 | convolution fusion | flops 1343225856 | bytes 4718592 | tf_op jit(solution)/shard_map/dot_general | solution.py:63
  175.1 3.7 %fusion = bf16[8,64,1920]{2,1,0:T(8,128)(2,1)} fusion(bf16[8,64,1920]{2,1,0:T(8,128)(2,1)} %collective-permute-done.4, pred[]{:T(512)S(6)} %eq.10, bf16[8,2,64,1920]{3,2,1,0:T(8,128)(2,1)S(1)} %bitcast.172), kind=kLoop, calls=%fused_computation.11 | loop fusion | flops 4915200 | bytes 7864321 | tf_op jit(solution)/shard_map/convert_element_type | solution.py:610
  178.7 20.9 %all-to-all-done.4.parts_ref = bf16[8,128,1152]{2,1,0:T(8,128)(2,1)S(1)} async-done(((bf16[8,128,1152]{2,1,0:T(8,128)(2,1)}), bf16[8,128,1152]{2,1,0:T(8,128)(2,1)S(1)}, u32[]{:S(2)}, u32[]{:S(2)}) %all-to-all-start.4) | async-done | bytes 2359328 | tf_op jit(solution)/shard_map/all_to_all | solution.py:27
  209.8 3.6 %all-to-all-start.5 = ((bf16[8,128,1024]{2,1,0:T(8,128)(2,1)}), bf16[8,128,1024]{2,1,0:T(8,128)(2,1)S(1)}, u32[]{:S(2)}, u32[]{:S(2)}) async-start(bf16[8,128,1024]{2,1,0:T(8,128)(2,1)} %broadcast_in_dim.87), calls=%async_computation.5 | async-start | bytes 4194304 | tf_op jit(solution)/shard_map/all_to_all | solution.py:27
  219.0 9.3 %reduce-scatter.2.cloned.1.call-done = bf16[128,1920]{1,0:T(8,128)(2,1)} async-done(((bf16[512,1920]{1,0:T(8,128)(2,1)}), bf16[128,1920]{1,0:T(8,128)(2,1)}) %reduce-scatter.2.cloned.1.call-update) | async-done | bytes 491536 | tf_op jit(solution)/shard_map/reduce_scatter | solution.py:631
  236.1 5.8 %all-to-all-done.5 = bf16[8,128,1024]{2,1,0:T(8,128)(2,1)S(1)} async-done(((bf16[8,128,1024]{2,1,0:T(8,128)(2,1)}), bf16[8,128,1024]{2,1,0:T(8,128)(2,1)S(1)}, u32[]{:S(2)}, u32[]{:S(2)}) %all-to-all-start.5) | async-done | bytes 2097184 | tf_op jit(solution)/shard_map/all_to_all | solution.py:27
  243.3 4.0 %collective-permute-start.7 = (bf16[64,1920]{1,0:T(8,128)(2,1)}, bf16[64,1920]{1,0:T(8,128)(2,1)}, u32[]{:S(2)}, u32[]{:S(2)}) collective-permute-start(bf16[64,1920]{1,0:T(8,128)(2,1)} %add_convert_fusion.1), channel_id=1, source_target_pairs={{0,16},{8,24},{16,0},{24,8},{32,48},{40,56},{48,32},{56,40},{64,80... | collective-permute-start | bytes 737288 | tf_op jit(solution)/shard_map/ppermute | solution.py:770
  247.3 4.5 %all-to-all-start.6 = ((bf16[8,128,1024]{2,1,0:T(8,128)(2,1)}), bf16[8,128,1024]{2,1,0:T(8,128)(2,1)}, u32[]{:S(2)}, u32[]{:S(2)}) async-start(bf16[8,128,1024]{2,1,0:T(8,128)(2,1)} %bitcast.185), calls=%async_computation.7 | async-start | bytes 4194304 | tf_op jit(solution)/shard_map/all_to_all | solution.py:27
  254.9 21.2 %attend_backward.1 = (f32[128,1024]{1,0:T(8,128)S(1)}, f32[128,1024]{1,0:T(8,128)S(1)}, bf16[128,1024]{1,0:T(8,128)(2,1)S(1)}) custom-call(s32[2,8]{1,0:T(2,128)S(1)} %pad_add_fusion.order_ref, bf16[128,1024]{1,0:T(8,128)(2,1)S(1)} %copy-done.28, bf16[2048,128]{1,0:T(8,128)(2,1)S(1)} %copy-done.30, bf16[128,2048]{1,0:T(8,128)(2,1)S(1)} %copy-done.32, ...), custom_call_target="tpu_custom_call" | custom-call | flops 23100000256 | bytes 63000000 | tf_op jit(solution)/shard_map/attend_backward/pallas_call | solution.py:218
  287.1 3.5 all-to-all-start.7
  294.5 4.5 %all-to-all-done.7 = bf16[8,64,512]{2,1,0:T(8,128)(2,1)S(1)} async-done(((bf16[8,64,512]{2,1,0:T(8,128)(2,1)}), bf16[8,64,512]{2,1,0:T(8,128)(2,1)S(1)}, u32[]{:S(2)}, u32[]{:S(2)}) %all-to-all-start.7) | async-done | bytes 524320 | tf_op jit(solution)/shard_map/all_to_all | solution.py:31
  300.3 6.5 %all-to-all-start.8 = ((bf16[8,512,128]{2,1,0:T(8,128)(2,1)}), bf16[8,512,128]{2,1,0:T(8,128)(2,1)S(1)}, u32[]{:S(2)}, u32[]{:S(2)}) async-start(bf16[8,512,128]{2,1,0:T(8,128)(2,1)} %pad_maximum_fusion.7), calls=%async_computation.9 | async-start | bytes 2097152 | tf_op jit(solution)/shard_map/all_to_all | solution.py:27
  306.8 4.2 %all-gather.6.cloned.1.call-done.gate_ref.up_ref.down_ref = bf16[8,64,1920]{2,1,0:T(8,128)(2,1)} async-done(((bf16[2,64,1920]{2,1,0:T(8,128)(2,1)}), bf16[8,64,1920]{2,1,0:T(8,128)(2,1)}) %all-gather.6.cloned.1.call-update) | async-done | bytes 1966096 | tf_op jit(solution)/shard_map/all_gather | solution.py:779
  315.1 5.1 %spread_experts.2 = (f32[10,128,1024]{2,1,0:T(8,128)}, f32[10,128,512]{2,1,0:T(8,128)}, f32[128,128]{1,0:T(8,128)S(1)}) custom-call(s32[2]{0:T(128)S(1)} %pad_add_fusion.1.place_ref, bf16[8,64,1920]{2,1,0:T(8,128)(2,1)S(1)} %copy-done.15, bf16[8,64,1920]{2,1,0:T(8,128)(2,1)S(1)} %copy-done.15, bf16[8,64,1920]{2,1,0:T(8,128)(2,1)S(1)} %copy-done.15, ...), custom_call_target="tpu_custom_call" | custom-call | flops 5500000256 | bytes 15000000 | tf_op jit(solution)/shard_map/spread_experts/pallas_call | solution.py:527
  323.8 3.5 collective-permute-start.10
  336.9 7.6 %spread_experts.3 = (f32[10,128,1024]{2,1,0:T(8,128)}, f32[10,128,512]{2,1,0:T(8,128)}, f32[128,128]{1,0:T(8,128)S(1)}) custom-call(s32[2]{0:T(128)S(1)} %pad_add_fusion.2.place_ref, bf16[8,64,1920]{2,1,0:T(8,128)(2,1)} %collective-permute-done.11.gate_ref.up_ref.down_ref, ...), custom_call_target="tpu_custom_call", output_to_operand_aliasing={{0}: (6, {}), {1}: (7, {}), {2}: (8, {})} | custom-call | flops 5500000256 | bytes 15000000 | tf_op jit(solution)/shard_map/spread_experts/pallas_call | solution.py:527
  (207 shorter events, 97.9 us)
Async XLA Ops:
  10.2 10.6 %collective-permute-start = (bf16[64,3072]{1,0:T(8,128)(2,1)S(1)}, bf16[64,3072]{1,0:T(8,128)(2,1)}, u32[]{:S(2)}, u32[]{:S(2)}) collective-permute-start(bf16[64,3072]{1,0:T(8,128)(2,1)S(1)} %get-tuple-element.170), channel_id=1, source_target_pairs={{0,4},{1,5},{2,6},{3,7},{4,0},{5,1},{6,2},{7,3},{8,12},{9,13},{10,... | collective-permute-start | bytes 1179656 | tf_op jit(solution)/shard_map/ppermute | solution.py:695
  13.8 15.4 %copy-start.5 = (bf16[1,128,1024]{2,1,0:T(8,128)(2,1)S(1)}, bf16[1,128,1024]{2,1,0:T(8,128)(2,1)}, u32[]{:S(2)}) copy-start(bf16[1,128,1024]{2,1,0:T(8,128)(2,1)} %param.11) | copy-start | bytes 786436
  14.8 14.4 %all-to-all-start = ((bf16[8,128,256]{2,1,0:T(8,128)(2,1)}), bf16[8,128,256]{2,1,0:T(8,128)(2,1)S(1)}, u32[]{:S(2)}, u32[]{:S(2)}) async-start(bf16[8,128,256]{2,1,0:T(8,128)(2,1)} %broadcast_in_dim.77), calls=%async_computation | async-start | bytes 1048576 | tf_op jit(solution)/shard_map/all_to_all | solution.py:31
  19.8 76.9 %all-gather.8.cloned.1.call-start = ((), (), s32[]{:S(2)}) async-start(), calls=%async_computation.12 | async-start | bytes 3932160 | tf_op jit(solution)/shard_map/all_gather | solution.py:614
  30.8 32.8 %all-to-all-start.1 = ((bf16[8,128,1024]{2,1,0:T(8,128)(2,1)}), bf16[8,128,1024]{2,1,0:T(8,128)(2,1)S(1)}, u32[]{:S(2)}, u32[]{:S(2)}) async-start(bf16[8,128,1024]{2,1,0:T(8,128)(2,1)} %broadcast_in_dim.79), calls=%async_computation.1 | async-start | bytes 4194304 | tf_op jit(solution)/shard_map/all_to_all | solution.py:27
  38.1 42.3 %collective-permute-start.2 = (bf16[64,2048]{1,0:T(8,128)(2,1)}, bf16[64,2048]{1,0:T(8,128)(2,1)}, u32[]{:S(2)}, u32[]{:S(2)}) collective-permute-start(bf16[64,2048]{1,0:T(8,128)(2,1)} %constant_dynamic-slice_fusion.1), channel_id=1, source_target_pairs={{0,4},{1,5},{2,6},{3,7},{4,0},{5,1},{6,2},{7,3},{8,12},{9,13},{10,... | collective-permute-start | bytes 786440 | tf_op jit(solution)/shard_map/ppermute | solution.py:697
  65.3 31.3 %all-to-all-start.2 = ((bf16[8,128,1152]{2,1,0:T(8,128)(2,1)}), bf16[8,128,1152]{2,1,0:T(8,128)(2,1)}, u32[]{:S(2)}, u32[]{:S(2)}) async-start(bf16[8,128,1152]{2,1,0:T(8,128)(2,1)} %broadcast_in_dim.80), calls=%async_computation.2 | async-start | bytes 4718592 | tf_op jit(solution)/shard_map/all_to_all | solution.py:27
  71.1 9.3 %copy-start.35 = (bf16[1,64,2048]{2,1,0:T(8,128)(2,1)S(1)}, bf16[1,64,2048]{2,1,0:T(8,128)(2,1)}, u32[]{:S(2)}) copy-start(bf16[1,64,2048]{2,1,0:T(8,128)(2,1)} %fusion.35) | copy-start | bytes 786436
  75.2 7.1 %collective-permute-start.1 = (bf16[128,1024]{1,0:T(8,128)(2,1)S(1)}, bf16[128,1024]{1,0:T(8,128)(2,1)S(1)}, u32[]{:S(2)}, u32[]{:S(2)}) collective-permute-start(bf16[128,1024]{1,0:T(8,128)(2,1)S(1)} %get-tuple-element.72.own_ref), channel_id=1, source_target_pairs={{0,8},{8,0},{16,24},{24,16},{32,40},{40,32},{48,56},{56,48},{64,72... | collective-permute-start | bytes 786440 | tf_op jit(solution)/shard_map/ppermute | solution.py:47
  96.7 12.9 %collective-permute-start.3 = (bf16[4,2,64,3072]{3,2,1,0:T(8,128)(2,1)}, bf16[4,2,64,3072]{3,2,1,0:T(8,128)(2,1)}, u32[]{:S(2)}, u32[]{:S(2)}) collective-permute-start(bf16[4,2,64,3072]{3,2,1,0:T(8,128)(2,1)} %bitcast.182), channel_id=1, source_target_pairs={{0,8},{8,0},{16,24},{24,16},{32,40},{40,32},{48,56},{56,48},{64,72... | collective-permute-start | bytes 9437192 | tf_op jit(solution)/shard_map/ppermute | solution.py:47
  104.4 33.0 %all-to-all-start.3 = ((bf16[8,1024,128]{2,1,0:T(8,128)(2,1)}), bf16[8,1024,128]{2,1,0:T(8,128)(2,1)}, u32[]{:S(2)}, u32[]{:S(2)}) async-start(bf16[8,1024,128]{2,1,0:T(8,128)(2,1)} %broadcast_in_dim.86), calls=%async_computation.3 | async-start | bytes 4194304 | tf_op jit(solution)/shard_map/all_to_all | solution.py:27
  108.8 55.9 %all-gather.10.cloned.1.call-start = ((), (), s32[]{:S(2)}) async-start(), calls=%async_computation.13 | async-start | bytes 2621440 | tf_op jit(solution)/shard_map/all_gather | solution.py:614
  163.9 11.2 %collective-permute-start.4 = (bf16[8,64,1920]{2,1,0:T(8,128)(2,1)}, bf16[8,64,1920]{2,1,0:T(8,128)(2,1)}, u32[]{:S(2)}, u32[]{:S(2)}) collective-permute-start(bf16[8,64,1920]{2,1,0:T(8,128)(2,1)} %fusion.9), channel_id=1, source_target_pairs={{0,8},{8,0},{16,24},{24,16},{32,40},{40,32},{48,56},{56,48},{64,72... | collective-permute-start | bytes 5898248 | tf_op jit(solution)/shard_map/ppermute | solution.py:47
  164.7 35.0 %all-to-all-start.4 = ((bf16[8,128,1152]{2,1,0:T(8,128)(2,1)}), bf16[8,128,1152]{2,1,0:T(8,128)(2,1)S(1)}, u32[]{:S(2)}, u32[]{:S(2)}) async-start(bf16[8,128,1152]{2,1,0:T(8,128)(2,1)} %bitcast.184), calls=%async_computation.4 | async-start | bytes 4718592 | tf_op jit(solution)/shard_map/all_to_all | solution.py:27
  168.3 60.0 %reduce-scatter.2.cloned.1.call-start = ((), (), s32[]{:S(2)}) async-start(), calls=%async_computation.10 | async-start | bytes 2457600 | tf_op jit(solution)/shard_map/reduce_scatter | solution.py:631
  203.1 10.3 %collective-permute-start.5 = (bf16[4,2,64,2048]{3,2,1,0:T(8,128)(2,1)}, bf16[4,2,64,2048]{3,2,1,0:T(8,128)(2,1)}, u32[]{:S(2)}, u32[]{:S(2)}) collective-permute-start(bf16[4,2,64,2048]{3,2,1,0:T(8,128)(2,1)} %bitcast.186), channel_id=1, source_target_pairs={{0,8},{8,0},{16,24},{24,16},{32,40},{40,32},{48,56},{56,48},{64,72... | collective-permute-start | bytes 6291464 | tf_op jit(solution)/shard_map/ppermute | solution.py:47
  209.8 32.1 %all-to-all-start.5 = ((bf16[8,128,1024]{2,1,0:T(8,128)(2,1)}), bf16[8,128,1024]{2,1,0:T(8,128)(2,1)S(1)}, u32[]{:S(2)}, u32[]{:S(2)}) async-start(bf16[8,128,1024]{2,1,0:T(8,128)(2,1)} %broadcast_in_dim.87), calls=%async_computation.5 | async-start | bytes 4194304 | tf_op jit(solution)/shard_map/all_to_all | solution.py:27
  230.0 12.5 %collective-permute-start.6 = (bf16[64,1920]{1,0:T(8,128)(2,1)}, bf16[64,1920]{1,0:T(8,128)(2,1)S(1)}, u32[]{:S(2)}, u32[]{:S(2)}) collective-permute-start(bf16[64,1920]{1,0:T(8,128)(2,1)} %slice.111), channel_id=1, source_target_pairs={{0,4},{1,5},{2,6},{3,7},{4,0},{5,1},{6,2},{7,3},{8,12},{9,13},{10,... | collective-permute-start | bytes 737288 | tf_op jit(solution)/shard_map/ppermute | solution.py:757
  233.8 8.8 %copy-start.36 = (bf16[128,1920]{1,0:T(8,128)(2,1)S(1)}, bf16[128,1920]{1,0:T(8,128)(2,1)}, u32[]{:S(2)}) copy-start(bf16[128,1920]{1,0:T(8,128)(2,1)} %reduce-scatter.2.cloned.1.call-done) | copy-start | bytes 1474564
  243.3 35.2 %collective-permute-start.7 = (bf16[64,1920]{1,0:T(8,128)(2,1)}, bf16[64,1920]{1,0:T(8,128)(2,1)}, u32[]{:S(2)}, u32[]{:S(2)}) collective-permute-start(bf16[64,1920]{1,0:T(8,128)(2,1)} %add_convert_fusion.1), channel_id=1, source_target_pairs={{0,16},{8,24},{16,0},{24,8},{32,48},{40,56},{48,32},{56,40},{64,80... | collective-permute-start | bytes 737288 | tf_op jit(solution)/shard_map/ppermute | solution.py:770
  247.3 33.0 %all-to-all-start.6 = ((bf16[8,128,1024]{2,1,0:T(8,128)(2,1)}), bf16[8,128,1024]{2,1,0:T(8,128)(2,1)}, u32[]{:S(2)}, u32[]{:S(2)}) async-start(bf16[8,128,1024]{2,1,0:T(8,128)(2,1)} %bitcast.185), calls=%async_computation.7 | async-start | bytes 4194304 | tf_op jit(solution)/shard_map/all_to_all | solution.py:27
  251.8 59.1 %all-gather.6.cloned.1.call-start = ((), (), s32[]{:S(2)}) async-start(), calls=%async_computation.11 | async-start | bytes 2457600 | tf_op jit(solution)/shard_map/all_gather | solution.py:779
  254.9 25.4 %copy-start.8 = (bf16[128,1024]{1,0:T(8,128)(2,1)S(1)}, bf16[128,1024]{1,0:T(8,128)(2,1)}, u32[]{:S(2)}) copy-start(bf16[128,1024]{1,0:T(8,128)(2,1)} %copy-done.7) | copy-start | bytes 786436
  254.9 25.4 %copy-start.12 = (bf16[128,128]{1,0:T(8,128)(2,1)S(1)}, bf16[128,128]{1,0:T(8,128)(2,1)}, u32[]{:S(2)}) copy-start(bf16[128,128]{1,0:T(8,128)(2,1)} %copy-done.11) | copy-start | bytes 98308
  280.7 2.4 collective-permute-start.8
  284.1 2.0 collective-permute-start.9
  287.1 11.9 %all-to-all-start.7 = ((bf16[8,64,512]{2,1,0:T(8,128)(2,1)}), bf16[8,64,512]{2,1,0:T(8,128)(2,1)S(1)}, u32[]{:S(2)}, u32[]{:S(2)}) async-start(bf16[8,64,512]{2,1,0:T(8,128)(2,1)} %fusion.15), calls=%async_computation.8 | async-start | bytes 1048576 | tf_op jit(solution)/shard_map/all_to_all | solution.py:31
  299.2 12.4 %copy-start.41 = (bf16[128]{0:T(256)(128)(2,1)S(1)}, bf16[128]{0:T(256)(128)(2,1)}, u32[]{:S(2)}) copy-start(bf16[128]{0:T(256)(128)(2,1)} %param.17) | copy-start | bytes 772
  300.3 21.3 %all-to-all-start.8 = ((bf16[8,512,128]{2,1,0:T(8,128)(2,1)}), bf16[8,512,128]{2,1,0:T(8,128)(2,1)S(1)}, u32[]{:S(2)}, u32[]{:S(2)}) async-start(bf16[8,512,128]{2,1,0:T(8,128)(2,1)} %pad_maximum_fusion.7), calls=%async_computation.9 | async-start | bytes 2097152 | tf_op jit(solution)/shard_map/all_to_all | solution.py:27
  311.0 24.2 %collective-permute-start.11 = (bf16[8,64,1920]{2,1,0:T(8,128)(2,1)}, bf16[8,64,1920]{2,1,0:T(8,128)(2,1)}, u32[]{:S(2)}, u32[]{:S(2)}) collective-permute-start(bf16[8,64,1920]{2,1,0:T(8,128)(2,1)} %all-gather.6.cloned.1.call-done.gate_ref.up_ref.down_ref), channel_id=1, source_target_pairs={{0,8},{8,0},{16,24},{24,16},{32,40},{40,32},{48,56},{56,48},{64,72... | collective-permute-start | bytes 5898248 | tf_op jit(solution)/shard_map/ppermute | solution.py:47
  323.8 8.4 %collective-permute-start.10 = (bf16[8,64,512]{2,1,0:T(8,128)(2,1)S(1)}, bf16[8,64,512]{2,1,0:T(8,128)(2,1)S(1)}, u32[]{:S(2)}, u32[]{:S(2)}) collective-permute-start(bf16[8,64,512]{2,1,0:T(8,128)(2,1)S(1)} %reshape.325.own_ref), channel_id=1, source_target_pairs={{0,8},{8,0},{16,24},{24,16},{32,40},{40,32},{48,56},{56,48},{64,72... | collective-permute-start | bytes 1572872 | tf_op jit(solution)/shard_map/ppermute | solution.py:47
  336.9 8.2 %copy-start.1 = (bf16[128,1024]{1,0:T(8,128)(2,1)S(1)}, bf16[128,1024]{1,0:T(8,128)(2,1)}, u32[]{:S(2)}) copy-start(bf16[128,1024]{1,0:T(8,128)(2,1)} %param.16) | copy-start | bytes 786436
  (36 other events, 94.6 us)
Sparse Core Ops, SparseCore 0:
  30.9 40.6 all-gather.7
  111.3 30.7 all-gather.9
  203.2 25.0 reduce-scatter.1
  280.5 30.4 all-gather.5

commit v3 on v2

--- a/solution.py
+++ b/solution.py
@@ -13,7 +13,7 @@
 NEGATIVE = -1e30
 BF16 = jnp.bfloat16
 F32 = jnp.float32
-VMEM_LIMIT = 48 * 1024 * 1024
+VMEM_LIMIT = 32 * 1024 * 1024
 
 GROUPS = [[2 * i + c for i in range(8)] for c in range(2)]
 PAIRS = [(i, i ^ 1) for i in range(16)]

time: 354 us -> 361 us (1.020)
  local copies, waits for them, and re-layouts: 46.6 us -> 60.4 us
    unnamed x95 -> x115, local copies, waits for them, and re-layouts: 22.9 us -> 35.2 us
    all_to_all x7, waiting for transfers between devices: 72.2 us -> 78.1 us  [exchange_ctx(): lax.all_to_all(parts, 'ctx', 0, 0, tiled=True, axis_index_groups=GROUPS)]
    reduce_scatter x1, waiting for transfers between devices: 9.31 us -> 3.53 us  [scatter_experts(): lax.psum_scatter(jnp.stack([mine, theirs], axis=1).reshape(512, parts.sha...]
  transfers between devices with their start and end apart: 25 -> 25, of which waited for: 14 -> 13; matrix products, arithmetic and copies ran while one was open for 19% -> 18% of each run, Pallas kernels for 18% -> 17%
where the time goes in v3:
time: 361 us; the launch traced here: 360 us
  waiting for transfers between devices  101 us (28%)
  starting transfers between devices  69.7 us (19%)
  Pallas kernels  67.6 us (19%)
  local copies, waits for them, and re-layouts  60.4 us (17%)
  other arithmetic  35.3 us (10%)
  between operations  14.5 us (4%)
  matrix products  11 us (3%)
    all_to_all x7, waiting for transfers between devices, exchange_ctx(): lax.all_to_all(parts, 'ctx', 0, 0, tiled=True, axis_index_groups=GROUPS)  78.1 us
    unnamed x115, local copies, waits for them, and re-layouts  35.2 us
    all_to_all x7, starting transfers between devices, exchange_ctx(): lax.all_to_all(parts, 'ctx', 0, 0, tiled=True, axis_index_groups=GROUPS)  34.7 us
    pallas_call x1, Pallas kernels, attend_backward(): pl.pallas_call(attend_back_kernel, out_shape=(jax.ShapeDtypeStruct((128,...  21 us
    ppermute x8, starting transfers between devices, swap_core(): return lax.ppermute(own, 'ctx', PAIRS)  18.5 us
    pallas_call x1, Pallas kernels, experts(): pl.pallas_call(experts_kernel, grid=(4,), out_shape=(jax.ShapeDtypeStruct...  15.4 us
    all_to_all x2, waiting for transfers between devices, exchange_fsdp(): return lax.all_to_all(parts, 'fsdp', 0, 0, tiled=True)  11.7 us
    pallas_call x1, Pallas kernels, attend_forward(): pl.pallas_call(attend_kernel, out_shape=(jax.ShapeDtypeStruct((1024, 128)...  10.7 us
  transfers between devices with their start and end apart: 25, of which 13 were waited for; matrix products, arithmetic and copies ran while one was open for 18% of the time, Pallas kernels for 17%

profile of v3, /device:TPU:1, one launch (start us, length us, event | category | flops | bytes accessed | tf_op | source)
XLA Modules:
  0.0 359.6 jit_solution(899225344351362546)
XLA Ops:
  14.8 5.0 %all-to-all-start = ((bf16[8,128,256]{2,1,0:T(8,128)(2,1)}), bf16[8,128,256]{2,1,0:T(8,128)(2,1)S(1)}, u32[]{:S(2)}, u32[]{:S(2)}) async-start(bf16[8,128,256]{2,1,0:T(8,128)(2,1)} %broadcast_in_dim.77), calls=%async_computation | async-start | bytes 1048576 | tf_op jit(solution)/shard_map/all_to_all | solution.py:31
  21.6 7.5 %all-to-all-done = bf16[8,128,256]{2,1,0:T(8,128)(2,1)S(1)} async-done(((bf16[8,128,256]{2,1,0:T(8,128)(2,1)}), bf16[8,128,256]{2,1,0:T(8,128)(2,1)S(1)}, u32[]{:S(2)}, u32[]{:S(2)}) %all-to-all-start) | async-done | bytes 524320 | tf_op jit(solution)/shard_map/all_to_all | solution.py:31
  30.8 6.8 %all-to-all-start.1 = ((bf16[8,128,1024]{2,1,0:T(8,128)(2,1)}), bf16[8,128,1024]{2,1,0:T(8,128)(2,1)S(1)}, u32[]{:S(2)}, u32[]{:S(2)}) async-start(bf16[8,128,1024]{2,1,0:T(8,128)(2,1)} %broadcast_in_dim.79), calls=%async_computation.1 | async-start | bytes 4194304 | tf_op jit(solution)/shard_map/all_to_all | solution.py:27
  39.5 24.3 %all-to-all-done.1 = bf16[8,128,1024]{2,1,0:T(8,128)(2,1)S(1)} async-done(((bf16[8,128,1024]{2,1,0:T(8,128)(2,1)}), bf16[8,128,1024]{2,1,0:T(8,128)(2,1)S(1)}, u32[]{:S(2)}, u32[]{:S(2)}) %all-to-all-start.1) | async-done | bytes 2097184 | tf_op jit(solution)/shard_map/all_to_all | solution.py:27
  65.9 5.2 %all-to-all-start.2 = ((bf16[8,128,1152]{2,1,0:T(8,128)(2,1)}), bf16[8,128,1152]{2,1,0:T(8,128)(2,1)S(1)}, u32[]{:S(2)}, u32[]{:S(2)}) async-start(bf16[8,128,1152]{2,1,0:T(8,128)(2,1)} %broadcast_in_dim.80), calls=%async_computation.2 | async-start | bytes 4718592 | tf_op jit(solution)/shard_map/all_to_all | solution.py:27
  77.4 4.5 %collective-permute-start.1 = (bf16[128,1024]{1,0:T(8,128)(2,1)S(1)}, bf16[128,1024]{1,0:T(8,128)(2,1)S(1)}, u32[]{:S(2)}, u32[]{:S(2)}) collective-permute-start(bf16[128,1024]{1,0:T(8,128)(2,1)S(1)} %get-tuple-element.72.own_ref), channel_id=1, source_target_pairs={{0,8},{8,0},{16,24},{24,16},{32,40},{40,32},{48,56},{56,48},{64,72... | collective-permute-start | bytes 786440 | tf_op jit(solution)/shard_map/ppermute | solution.py:47
  85.6 10.7 %attend_forward.1 = (bf16[1024,128]{1,0:T(8,128)(2,1)S(1)}, bf16[2048,128]{1,0:T(8,128)(2,1)S(1)}, bf16[128,2048]{1,0:T(8,128)(2,1)S(1)}) custom-call(s32[2,8]{1,0:T(2,128)S(1)} %pad_add_fusion.order_ref, bf16[128,1024]{1,0:T(8,128)(2,1)S(1)} %copy-done.36, bf16[128,1024]{1,0:T(8,128)(2,1)S(1)} %copy-done.27, ...), custom_call_target="tpu_custom_call" | custom-call | flops 12099999744 | bytes 33000000 | tf_op jit(solution)/shard_map/attend_forward/pallas_call | solution.py:127
  97.9 5.3 %collective-permute-start.3 = (bf16[4,2,64,3072]{3,2,1,0:T(8,128)(2,1)}, bf16[4,2,64,3072]{3,2,1,0:T(8,128)(2,1)}, u32[]{:S(2)}, u32[]{:S(2)}) collective-permute-start(bf16[4,2,64,3072]{3,2,1,0:T(8,128)(2,1)} %bitcast.186), channel_id=1, source_target_pairs={{0,8},{8,0},{16,24},{24,16},{32,40},{40,32},{48,56},{56,48},{64,72... | collective-permute-start | bytes 9437192 | tf_op jit(solution)/shard_map/ppermute | solution.py:47
  104.8 4.3 %all-to-all-start.3 = ((bf16[8,1024,128]{2,1,0:T(8,128)(2,1)}), bf16[8,1024,128]{2,1,0:T(8,128)(2,1)}, u32[]{:S(2)}, u32[]{:S(2)}) async-start(bf16[8,1024,128]{2,1,0:T(8,128)(2,1)} %broadcast_in_dim.86), calls=%async_computation.3 | async-start | bytes 4194304 | tf_op jit(solution)/shard_map/all_to_all | solution.py:27
  109.9 3.3 select_bitcast_fusion.1
  115.0 3.1 copy.89
  118.1 19.7 %all-to-all-done.3.attended_ref = bf16[8,1024,128]{2,1,0:T(8,128)(2,1)} async-done(((bf16[8,1024,128]{2,1,0:T(8,128)(2,1)}), bf16[8,1024,128]{2,1,0:T(8,128)(2,1)}, u32[]{:S(2)}, u32[]{:S(2)}) %all-to-all-start.3) | async-done | bytes 2097184 | tf_op jit(solution)/shard_map/all_to_all | solution.py:27
  139.4 15.4 %experts.1 = (f32[1024,1024]{1,0:T(8,128)S(1)}, f32[1024,128]{1,0:T(8,128)S(1)}, bf16[1024,1024]{1,0:T(8,128)(2,1)S(1)}, bf16[1024,640]{1,0:T(8,128)(2,1)S(1)}, ...) custom-call(s32[1]{0:T(128)} %bitcast.11.first_ref, bf16[1024,1024]{1,0:T(8,128)(2,1)S(1)} %bitcast.172, ...), custom_call_target="tpu_custom_call" | custom-call | flops 17600000000 | bytes 48000000 | tf_op jit(solution)/shard_map/experts/pallas_call | solution.py:352
  158.0 3.2 convolution_convert_fusion
  164.9 4.4 %all-to-all-start.4 = ((bf16[8,128,1152]{2,1,0:T(8,128)(2,1)}), bf16[8,128,1152]{2,1,0:T(8,128)(2,1)}, u32[]{:S(2)}, u32[]{:S(2)}) async-start(bf16[8,128,1152]{2,1,0:T(8,128)(2,1)} %bitcast.170), calls=%async_computation.4 | async-start | bytes 4718592 | tf_op jit(solution)/shard_map/all_to_all | solution.py:27
  171.0 5.0 %convolution_convert_fusion.1 = bf16[1024,1024]{1,0:T(8,128)(2,1)} fusion(bf16[1024,640]{1,0:T(8,128)(2,1)} %copy-done.30, bf16[1024,3072]{1,0:T(8,128)(2,1)} %bitcast.162), kind=kOutput, calls=%fused_computation.34 | convolution fusion | flops 1343225856 | bytes 4718592 | tf_op jit(solution)/shard_map/dot_general | solution.py:63
  176.1 3.7 %fusion = bf16[8,64,1920]{2,1,0:T(8,128)(2,1)} fusion(bf16[8,64,1920]{2,1,0:T(8,128)(2,1)} %collective-permute-done.4, pred[]{:T(512)S(6)} %eq.10, bf16[8,2,64,1920]{3,2,1,0:T(8,128)(2,1)S(1)} %bitcast.180), kind=kLoop, calls=%fused_computation.11 | loop fusion | flops 4915200 | bytes 7864321 | tf_op jit(solution)/shard_map/convert_element_type | solution.py:610
  179.7 21.0 %all-to-all-done.4.parts_ref = bf16[8,128,1152]{2,1,0:T(8,128)(2,1)} async-done(((bf16[8,128,1152]{2,1,0:T(8,128)(2,1)}), bf16[8,128,1152]{2,1,0:T(8,128)(2,1)}, u32[]{:S(2)}, u32[]{:S(2)}) %all-to-all-start.4) | async-done | bytes 2359328 | tf_op jit(solution)/shard_map/all_to_all | solution.py:27
  205.2 2.8 copy-done.2
  216.6 3.6 %all-to-all-start.5 = ((bf16[8,128,1024]{2,1,0:T(8,128)(2,1)}), bf16[8,128,1024]{2,1,0:T(8,128)(2,1)S(1)}, u32[]{:S(2)}, u32[]{:S(2)}) async-start(bf16[8,128,1024]{2,1,0:T(8,128)(2,1)} %broadcast_in_dim.87), calls=%async_computation.5 | async-start | bytes 4194304 | tf_op jit(solution)/shard_map/all_to_all | solution.py:27
  225.9 3.5 reduce-scatter.2.cloned.1.call-done
  237.2 11.7 %all-to-all-done.5 = bf16[8,128,1024]{2,1,0:T(8,128)(2,1)S(1)} async-done(((bf16[8,128,1024]{2,1,0:T(8,128)(2,1)}), bf16[8,128,1024]{2,1,0:T(8,128)(2,1)S(1)}, u32[]{:S(2)}, u32[]{:S(2)}) %all-to-all-start.5) | async-done | bytes 2097184 | tf_op jit(solution)/shard_map/all_to_all | solution.py:27
  249.9 4.0 %collective-permute-start.7 = (bf16[64,1920]{1,0:T(8,128)(2,1)}, bf16[64,1920]{1,0:T(8,128)(2,1)}, u32[]{:S(2)}, u32[]{:S(2)}) collective-permute-start(bf16[64,1920]{1,0:T(8,128)(2,1)} %add_convert_fusion.1), channel_id=1, source_target_pairs={{0,16},{8,24},{16,0},{24,8},{32,48},{40,56},{48,32},{56,40},{64,80... | collective-permute-start | bytes 737288 | tf_op jit(solution)/shard_map/ppermute | solution.py:770
  253.9 4.5 %all-to-all-start.6 = ((bf16[8,128,1024]{2,1,0:T(8,128)(2,1)}), bf16[8,128,1024]{2,1,0:T(8,128)(2,1)}, u32[]{:S(2)}, u32[]{:S(2)}) async-start(bf16[8,128,1024]{2,1,0:T(8,128)(2,1)} %bitcast.188), calls=%async_computation.7 | async-start | bytes 4194304 | tf_op jit(solution)/shard_map/all_to_all | solution.py:27
  261.5 21.0 %attend_backward.1 = (f32[128,1024]{1,0:T(8,128)S(1)}, f32[128,1024]{1,0:T(8,128)S(1)}, bf16[128,1024]{1,0:T(8,128)(2,1)S(1)}) custom-call(s32[2,8]{1,0:T(2,128)S(1)} %pad_add_fusion.order_ref, bf16[128,1024]{1,0:T(8,128)(2,1)S(1)} %copy-done.37, bf16[2048,128]{1,0:T(8,128)(2,1)S(1)} %copy-done.39, bf16[128,2048]{1,0:T(8,128)(2,1)S(1)} %copy-done.41, ...), custom_call_target="tpu_custom_call" | custom-call | flops 23100000256 | bytes 63000000 | tf_op jit(solution)/shard_map/attend_backward/pallas_call | solution.py:218
  293.7 3.8 %all-to-all-start.7 = ((bf16[8,64,512]{2,1,0:T(8,128)(2,1)}), bf16[8,64,512]{2,1,0:T(8,128)(2,1)S(1)}, u32[]{:S(2)}, u32[]{:S(2)}) async-start(bf16[8,64,512]{2,1,0:T(8,128)(2,1)} %fusion.15), calls=%async_computation.8 | async-start | bytes 1048576 | tf_op jit(solution)/shard_map/all_to_all | solution.py:31
  301.5 4.2 %all-to-all-done.7 = bf16[8,64,512]{2,1,0:T(8,128)(2,1)S(1)} async-done(((bf16[8,64,512]{2,1,0:T(8,128)(2,1)}), bf16[8,64,512]{2,1,0:T(8,128)(2,1)S(1)}, u32[]{:S(2)}, u32[]{:S(2)}) %all-to-all-start.7) | async-done | bytes 524320 | tf_op jit(solution)/shard_map/all_to_all | solution.py:31
  306.9 6.0 %all-to-all-start.8 = ((bf16[8,512,128]{2,1,0:T(8,128)(2,1)}), bf16[8,512,128]{2,1,0:T(8,128)(2,1)S(1)}, u32[]{:S(2)}, u32[]{:S(2)}) async-start(bf16[8,512,128]{2,1,0:T(8,128)(2,1)} %pad_maximum_fusion.7), calls=%async_computation.9 | async-start | bytes 2097152 | tf_op jit(solution)/shard_map/all_to_all | solution.py:27
  312.9 4.0 %all-gather.6.cloned.1.call-done.gate_ref.up_ref.down_ref = bf16[8,64,1920]{2,1,0:T(8,128)(2,1)} async-done(((bf16[2,64,1920]{2,1,0:T(8,128)(2,1)}), bf16[8,64,1920]{2,1,0:T(8,128)(2,1)}) %all-gather.6.cloned.1.call-update) | async-done | bytes 1966096 | tf_op jit(solution)/shard_map/all_gather | solution.py:779
  321.1 5.1 %spread_experts.2 = (f32[10,128,1024]{2,1,0:T(8,128)}, f32[10,128,512]{2,1,0:T(8,128)}, f32[128,128]{1,0:T(8,128)S(1)}) custom-call(s32[2]{0:T(128)S(1)} %pad_add_fusion.1.place_ref, bf16[8,64,1920]{2,1,0:T(8,128)(2,1)S(1)} %copy-done.23, bf16[8,64,1920]{2,1,0:T(8,128)(2,1)S(1)} %copy-done.23, bf16[8,64,1920]{2,1,0:T(8,128)(2,1)S(1)} %copy-done.23, ...), custom_call_target="tpu_custom_call" | custom-call | flops 5500000256 | bytes 15000000 | tf_op jit(solution)/shard_map/spread_experts/pallas_call | solution.py:527
  332.1 3.5 collective-permute-start.10
  347.3 5.1 %spread_experts.3 = (f32[10,128,1024]{2,1,0:T(8,128)}, f32[10,128,512]{2,1,0:T(8,128)}, f32[128,128]{1,0:T(8,128)S(1)}) custom-call(s32[2]{0:T(128)S(1)} %pad_add_fusion.2.place_ref, bf16[8,64,1920]{2,1,0:T(8,128)(2,1)S(1)} %collective-permute-done.11.gate_ref.up_ref.down_ref, ...), custom_call_target="tpu_custom_call", output_to_operand_aliasing={{0}: (6, {}), {1}: (7, {}), {2}: (8, {})} | custom-call | flops 5500000256 | bytes 15000000 | tf_op jit(solution)/shard_map/spread_experts/pallas_call | solution.py:527
  (227 shorter events, 109.9 us)
Async XLA Ops:
  10.2 10.5 %collective-permute-start = (bf16[64,3072]{1,0:T(8,128)(2,1)S(1)}, bf16[64,3072]{1,0:T(8,128)(2,1)S(1)}, u32[]{:S(2)}, u32[]{:S(2)}) collective-permute-start(bf16[64,3072]{1,0:T(8,128)(2,1)S(1)} %get-tuple-element.170), channel_id=1, source_target_pairs={{0,4},{1,5},{2,6},{3,7},{4,0},{5,1},{6,2},{7,3},{8,12},{9,13},{10,... | collective-permute-start | bytes 1179656 | tf_op jit(solution)/shard_map/ppermute | solution.py:695
  13.8 15.4 %copy-start.12 = (bf16[1,128,1024]{2,1,0:T(8,128)(2,1)S(1)}, bf16[1,128,1024]{2,1,0:T(8,128)(2,1)}, u32[]{:S(2)}) copy-start(bf16[1,128,1024]{2,1,0:T(8,128)(2,1)} %param.11) | copy-start | bytes 786436
  14.8 14.4 %all-to-all-start = ((bf16[8,128,256]{2,1,0:T(8,128)(2,1)}), bf16[8,128,256]{2,1,0:T(8,128)(2,1)S(1)}, u32[]{:S(2)}, u32[]{:S(2)}) async-start(bf16[8,128,256]{2,1,0:T(8,128)(2,1)} %broadcast_in_dim.77), calls=%async_computation | async-start | bytes 1048576 | tf_op jit(solution)/shard_map/all_to_all | solution.py:31
  19.8 78.1 %all-gather.8.cloned.1.call-start = ((), (), s32[]{:S(2)}) async-start(), calls=%async_computation.12 | async-start | bytes 3932160 | tf_op jit(solution)/shard_map/all_gather | solution.py:614
  30.8 33.0 %all-to-all-start.1 = ((bf16[8,128,1024]{2,1,0:T(8,128)(2,1)}), bf16[8,128,1024]{2,1,0:T(8,128)(2,1)S(1)}, u32[]{:S(2)}, u32[]{:S(2)}) async-start(bf16[8,128,1024]{2,1,0:T(8,128)(2,1)} %broadcast_in_dim.79), calls=%async_computation.1 | async-start | bytes 4194304 | tf_op jit(solution)/shard_map/all_to_all | solution.py:27
  38.3 43.6 %collective-permute-start.2 = (bf16[64,2048]{1,0:T(8,128)(2,1)}, bf16[64,2048]{1,0:T(8,128)(2,1)}, u32[]{:S(2)}, u32[]{:S(2)}) collective-permute-start(bf16[64,2048]{1,0:T(8,128)(2,1)} %constant_dynamic-slice_fusion.1), channel_id=1, source_target_pairs={{0,4},{1,5},{2,6},{3,7},{4,0},{5,1},{6,2},{7,3},{8,12},{9,13},{10,... | collective-permute-start | bytes 786440 | tf_op jit(solution)/shard_map/ppermute | solution.py:697
  65.9 32.0 %all-to-all-start.2 = ((bf16[8,128,1152]{2,1,0:T(8,128)(2,1)}), bf16[8,128,1152]{2,1,0:T(8,128)(2,1)S(1)}, u32[]{:S(2)}, u32[]{:S(2)}) async-start(bf16[8,128,1152]{2,1,0:T(8,128)(2,1)} %broadcast_in_dim.80), calls=%async_computation.2 | async-start | bytes 4718592 | tf_op jit(solution)/shard_map/all_to_all | solution.py:27
  77.4 6.3 %collective-permute-start.1 = (bf16[128,1024]{1,0:T(8,128)(2,1)S(1)}, bf16[128,1024]{1,0:T(8,128)(2,1)S(1)}, u32[]{:S(2)}, u32[]{:S(2)}) collective-permute-start(bf16[128,1024]{1,0:T(8,128)(2,1)S(1)} %get-tuple-element.72.own_ref), channel_id=1, source_target_pairs={{0,8},{8,0},{16,24},{24,16},{32,40},{40,32},{48,56},{56,48},{64,72... | collective-permute-start | bytes 786440 | tf_op jit(solution)/shard_map/ppermute | solution.py:47
  97.9 12.0 %collective-permute-start.3 = (bf16[4,2,64,3072]{3,2,1,0:T(8,128)(2,1)}, bf16[4,2,64,3072]{3,2,1,0:T(8,128)(2,1)}, u32[]{:S(2)}, u32[]{:S(2)}) collective-permute-start(bf16[4,2,64,3072]{3,2,1,0:T(8,128)(2,1)} %bitcast.186), channel_id=1, source_target_pairs={{0,8},{8,0},{16,24},{24,16},{32,40},{40,32},{48,56},{56,48},{64,72... | collective-permute-start | bytes 9437192 | tf_op jit(solution)/shard_map/ppermute | solution.py:47
  104.8 33.0 %all-to-all-start.3 = ((bf16[8,1024,128]{2,1,0:T(8,128)(2,1)}), bf16[8,1024,128]{2,1,0:T(8,128)(2,1)}, u32[]{:S(2)}, u32[]{:S(2)}) async-start(bf16[8,1024,128]{2,1,0:T(8,128)(2,1)} %broadcast_in_dim.86), calls=%async_computation.3 | async-start | bytes 4194304 | tf_op jit(solution)/shard_map/all_to_all | solution.py:27
  109.2 55.7 %all-gather.10.cloned.1.call-start = ((), (), s32[]{:S(2)}) async-start(), calls=%async_computation.13 | async-start | bytes 2621440 | tf_op jit(solution)/shard_map/all_gather | solution.py:614
  164.1 12.0 %collective-permute-start.4 = (bf16[8,64,1920]{2,1,0:T(8,128)(2,1)}, bf16[8,64,1920]{2,1,0:T(8,128)(2,1)}, u32[]{:S(2)}, u32[]{:S(2)}) collective-permute-start(bf16[8,64,1920]{2,1,0:T(8,128)(2,1)} %fusion.9), channel_id=1, source_target_pairs={{0,8},{8,0},{16,24},{24,16},{32,40},{40,32},{48,56},{56,48},{64,72... | collective-permute-start | bytes 5898248 | tf_op jit(solution)/shard_map/ppermute | solution.py:47
  164.9 35.8 %all-to-all-start.4 = ((bf16[8,128,1152]{2,1,0:T(8,128)(2,1)}), bf16[8,128,1152]{2,1,0:T(8,128)(2,1)}, u32[]{:S(2)}, u32[]{:S(2)}) async-start(bf16[8,128,1152]{2,1,0:T(8,128)(2,1)} %bitcast.170), calls=%async_computation.4 | async-start | bytes 4718592 | tf_op jit(solution)/shard_map/all_to_all | solution.py:27
  169.3 60.1 %reduce-scatter.2.cloned.1.call-start = ((), (), s32[]{:S(2)}) async-start(), calls=%async_computation.10 | async-start | bytes 2457600 | tf_op jit(solution)/shard_map/reduce_scatter | solution.py:631
  204.1 16.1 %collective-permute-start.5 = (bf16[4,2,64,2048]{3,2,1,0:T(8,128)(2,1)}, bf16[4,2,64,2048]{3,2,1,0:T(8,128)(2,1)}, u32[]{:S(2)}, u32[]{:S(2)}) collective-permute-start(bf16[4,2,64,2048]{3,2,1,0:T(8,128)(2,1)} %bitcast.189), channel_id=1, source_target_pairs={{0,8},{8,0},{16,24},{24,16},{32,40},{40,32},{48,56},{56,48},{64,72... | collective-permute-start | bytes 6291464 | tf_op jit(solution)/shard_map/ppermute | solution.py:47
  216.6 32.3 %all-to-all-start.5 = ((bf16[8,128,1024]{2,1,0:T(8,128)(2,1)}), bf16[8,128,1024]{2,1,0:T(8,128)(2,1)S(1)}, u32[]{:S(2)}, u32[]{:S(2)}) async-start(bf16[8,128,1024]{2,1,0:T(8,128)(2,1)} %broadcast_in_dim.87), calls=%async_computation.5 | async-start | bytes 4194304 | tf_op jit(solution)/shard_map/all_to_all | solution.py:27
  231.0 18.1 %collective-permute-start.6 = (bf16[64,1920]{1,0:T(8,128)(2,1)}, bf16[64,1920]{1,0:T(8,128)(2,1)S(1)}, u32[]{:S(2)}, u32[]{:S(2)}) collective-permute-start(bf16[64,1920]{1,0:T(8,128)(2,1)} %slice.111), channel_id=1, source_target_pairs={{0,4},{1,5},{2,6},{3,7},{4,0},{5,1},{6,2},{7,3},{8,12},{9,13},{10,... | collective-permute-start | bytes 737288 | tf_op jit(solution)/shard_map/ppermute | solution.py:757
  234.9 14.3 %copy-start.46 = (bf16[128,1920]{1,0:T(8,128)(2,1)S(1)}, bf16[128,1920]{1,0:T(8,128)(2,1)}, u32[]{:S(2)}) copy-start(bf16[128,1920]{1,0:T(8,128)(2,1)} %reduce-scatter.2.cloned.1.call-done) | copy-start | bytes 1474564
  249.9 34.3 %collective-permute-start.7 = (bf16[64,1920]{1,0:T(8,128)(2,1)}, bf16[64,1920]{1,0:T(8,128)(2,1)}, u32[]{:S(2)}, u32[]{:S(2)}) collective-permute-start(bf16[64,1920]{1,0:T(8,128)(2,1)} %add_convert_fusion.1), channel_id=1, source_target_pairs={{0,16},{8,24},{16,0},{24,8},{32,48},{40,56},{48,32},{56,40},{64,80... | collective-permute-start | bytes 737288 | tf_op jit(solution)/shard_map/ppermute | solution.py:770
  253.9 32.1 %all-to-all-start.6 = ((bf16[8,128,1024]{2,1,0:T(8,128)(2,1)}), bf16[8,128,1024]{2,1,0:T(8,128)(2,1)}, u32[]{:S(2)}, u32[]{:S(2)}) async-start(bf16[8,128,1024]{2,1,0:T(8,128)(2,1)} %bitcast.188), calls=%async_computation.7 | async-start | bytes 4194304 | tf_op jit(solution)/shard_map/all_to_all | solution.py:27
  258.4 58.5 %all-gather.6.cloned.1.call-start = ((), (), s32[]{:S(2)}) async-start(), calls=%async_computation.11 | async-start | bytes 2457600 | tf_op jit(solution)/shard_map/all_gather | solution.py:779
  261.5 24.6 %copy-start.16 = (bf16[128,1024]{1,0:T(8,128)(2,1)S(1)}, bf16[128,1024]{1,0:T(8,128)(2,1)}, u32[]{:S(2)}) copy-start(bf16[128,1024]{1,0:T(8,128)(2,1)} %copy-done.15) | copy-start | bytes 786436
  261.5 24.6 %copy-start.20 = (bf16[128,128]{1,0:T(8,128)(2,1)S(1)}, bf16[128,128]{1,0:T(8,128)(2,1)}, u32[]{:S(2)}) copy-start(bf16[128,128]{1,0:T(8,128)(2,1)} %copy-done.19) | copy-start | bytes 98308
  286.4 3.1 collective-permute-start.8
  290.5 2.2 collective-permute-start.9
  293.7 11.9 %all-to-all-start.7 = ((bf16[8,64,512]{2,1,0:T(8,128)(2,1)}), bf16[8,64,512]{2,1,0:T(8,128)(2,1)S(1)}, u32[]{:S(2)}, u32[]{:S(2)}) async-start(bf16[8,64,512]{2,1,0:T(8,128)(2,1)} %fusion.15), calls=%async_computation.8 | async-start | bytes 1048576 | tf_op jit(solution)/shard_map/all_to_all | solution.py:31
  305.8 11.8 %copy-start.52 = (bf16[128]{0:T(256)(128)(2,1)S(1)}, bf16[128]{0:T(256)(128)(2,1)}, u32[]{:S(2)}) copy-start(bf16[128]{0:T(256)(128)(2,1)} %param.17) | copy-start | bytes 772
  306.9 20.8 %all-to-all-start.8 = ((bf16[8,512,128]{2,1,0:T(8,128)(2,1)}), bf16[8,512,128]{2,1,0:T(8,128)(2,1)S(1)}, u32[]{:S(2)}, u32[]{:S(2)}) async-start(bf16[8,512,128]{2,1,0:T(8,128)(2,1)} %pad_maximum_fusion.7), calls=%async_computation.9 | async-start | bytes 2097152 | tf_op jit(solution)/shard_map/all_to_all | solution.py:27
  317.0 28.6 %collective-permute-start.11 = (bf16[8,64,1920]{2,1,0:T(8,128)(2,1)}, bf16[8,64,1920]{2,1,0:T(8,128)(2,1)S(1)}, u32[]{:S(2)}, u32[]{:S(2)}) collective-permute-start(bf16[8,64,1920]{2,1,0:T(8,128)(2,1)} %all-gather.6.cloned.1.call-done.gate_ref.up_ref.down_ref), channel_id=1, source_target_pairs={{0,8},{8,0},{16,24},{24,16},{32,40},{40,32},{48,56},{56,48},{64,72... | collective-permute-start | bytes 5898248 | tf_op jit(solution)/shard_map/ppermute | solution.py:47
  326.2 9.3 %copy-start.48 = (bf16[128,10]{0,1:T(8,128)(2,1)S(1)}, bf16[128,10]{0,1:T(8,128)(2,1)}, u32[]{:S(2)}) copy-start(bf16[128,10]{0,1:T(8,128)(2,1)} %param.18) | copy-start | bytes 7684
  326.2 9.6 %copy-start.13 = (bf16[1,128,1024]{2,1,0:T(8,128)(2,1)S(1)}, bf16[1,128,1024]{2,1,0:T(8,128)(2,1)}, u32[]{:S(2)}) copy-start(bf16[1,128,1024]{2,1,0:T(8,128)(2,1)} %param.11) | copy-start | bytes 786436
  332.1 9.4 %collective-permute-start.10 = (bf16[8,64,512]{2,1,0:T(8,128)(2,1)S(1)}, bf16[8,64,512]{2,1,0:T(8,128)(2,1)}, u32[]{:S(2)}, u32[]{:S(2)}) collective-permute-start(bf16[8,64,512]{2,1,0:T(8,128)(2,1)S(1)} %reshape.325.own_ref), channel_id=1, source_target_pairs={{0,8},{8,0},{16,24},{24,16},{32,40},{40,32},{48,56},{56,48},{64,72... | collective-permute-start | bytes 1572872 | tf_op jit(solution)/shard_map/ppermute | solution.py:47
  (46 other events, 123.9 us)
Sparse Core Ops, SparseCore 0:
  30.9 40.6 all-gather.7
  111.7 30.8 all-gather.9
  204.2 25.1 reduce-scatter.1
  286.2 30.7 all-gather.5
